TPU v7x, 32 devices: a whole 2x2x4 slice. The times are simulated.
32 devices in a mesh: pipe: 2 (over x), dp: 16 (over z, y, core).
Axes of the slice: x: 2, y: 2, z: 4, core: 2. Of those that a mesh axis runs over, the one named last changes fastest.
Arguments:
- tokens: bfloat16 [512, 6144], P(('pipe', 'dp')), may hold values from -6 to 6
- cotangent: bfloat16 [512, 6144], P(('pipe', 'dp')), may hold values from -6 to 6
- norm_gain: float32 [2, 6144], P('pipe'), may hold values from 0.5 to 1.5
- up_blocks: float32 [2, 4, 96, 384], P('pipe'), may hold values from -0.625 to 0.625
- down_blocks: float32 [2, 4, 96, 384], P('pipe'), may hold values from -0.3125 to 0.3125
- up_left: float32 [2, 8, 6144], P('pipe'), may hold values from -0.078125 to 0.078125
- up_right: float32 [2, 8, 24576], P('pipe'), may hold values from -2 to 2
- down_left: float32 [2, 8, 24576], P('pipe'), may hold values from -0.0390625 to 0.0390625
- down_right: float32 [2, 8, 6144], P('pipe'), may hold values from -2 to 2
- block_pattern: int32 [2, 2, 2, 4], P('pipe'), may hold values from 0 to 63, as said below
- rank_used: int32 [2, 2], P('pipe'), may hold values from 1 to 8
Outputs:
- final_tokens: bfloat16 [512, 6144], P(('pipe', 'dp'))
- input_gradient: bfloat16 [512, 6144], P(('pipe', 'dp'))
- grad_up_blocks: float32 [2, 4, 96, 384], P('pipe', None, None, 'dp')
- grad_down_blocks: float32 [2, 4, 96, 384], P('pipe', None, None, 'dp')
- grad_up_left: float32 [2, 8, 6144], P('pipe', None, 'dp')
- grad_up_right: float32 [2, 8, 24576], P('pipe', None, 'dp')
- grad_down_left: float32 [2, 8, 24576], P('pipe', None, 'dp')
- grad_down_right: float32 [2, 8, 6144], P('pipe', None, 'dp')
- grad_gain: float32 [2, 6144], P('pipe', 'dp')
Inputs may be any that keep to these rules, and one draw needn't show every extreme that they name: block_pattern[l, p, 1, k] is block_pattern[l, p, 0, k] with exactly one of its 6 bits flipped (a butterfly pair); pairs may repeat.
All inputs are finite; a program needn't handle non-finite values.
Results may differ from a plain program's by a relative error of at most 0.0052.
Values may be sent and summed in bfloat16 or wider, within the bound.
A program may use at most 128 MiB of HBM per device.

v0:
```python
import math

import jax
import jax.numpy as jnp
from jax import lax
from jax.sharding import PartitionSpec as P

precise = lax.Precision.HIGHEST


def from_behind(block, axis, distance):
    devices = range(lax.axis_size(axis))
    route = [(i - distance, i) for i in devices if i - distance in devices]
    return lax.ppermute(block, axis, route)


def gelu_tanh(value):
    return (
        0.5
        * value
        * (1.0 + jnp.tanh(0.7978845608028654 * (value + 0.044715 * value * value * value)))
    )


def selector(indices, group_count):
    groups = jnp.arange(group_count, dtype=jnp.int32)
    return jnp.where(indices[:, None] == groups[None, :], 1.0, 0.0).astype(jnp.float32)


def layer_apply(act, params, pattern, ranks):
    up_blocks, down_blocks, up_left, up_right, down_left, down_right, gain = params
    token_count = act.shape[0]
    feature_width = act.shape[1]
    block_feat = up_blocks.shape[1]
    block_hidden = up_blocks.shape[2]
    group_count = feature_width // block_feat
    hidden_width = up_right.shape[1]
    rank_index = jnp.arange(up_left.shape[0], dtype=jnp.int32)
    up_mask = jnp.where(rank_index < ranks[0], 1.0, 0.0).astype(jnp.float32)
    down_mask = jnp.where(rank_index < ranks[1], 1.0, 0.0).astype(jnp.float32)
    up_source = selector(pattern[0, 0], group_count)
    up_target = selector(pattern[0, 1], group_count)
    down_source = selector(pattern[1, 0], group_count)
    down_target = selector(pattern[1, 1], group_count)
    mean_square = jnp.mean(act * act, axis=1, keepdims=True)
    normed = act * lax.rsqrt(mean_square + 1e-05) * gain
    pieces = jnp.einsum(
        "rgd,kg->rkd",
        normed.reshape(token_count, group_count, block_feat),
        up_source,
        precision=precise,
    )
    up_parts = jnp.einsum("rkd,kdf->rkf", pieces, up_blocks, precision=precise)
    low_coeff = jnp.einsum("rd,qd->rq", normed, up_left, precision=precise) * up_mask
    hidden = jnp.einsum("rq,qf->rf", low_coeff, up_right, precision=precise).reshape(
        token_count, group_count, block_hidden
    )
    hidden = gelu_tanh(hidden + jnp.einsum("rkf,kg->rgf", up_parts, up_target, precision=precise))
    hidden_pieces = jnp.einsum("rgf,kg->rkf", hidden, down_source, precision=precise)
    down_parts = jnp.einsum("rkf,kdf->rkd", hidden_pieces, down_blocks, precision=precise)
    flat_hidden = hidden.reshape(token_count, hidden_width)
    low_down = jnp.einsum("rf,qf->rq", flat_hidden, down_left, precision=precise) * down_mask
    branch = jnp.einsum("rq,qd->rd", low_down, down_right, precision=precise)
    placed = jnp.einsum("rkd,kg->rgd", down_parts, down_target, precision=precise).reshape(
        token_count, feature_width
    )
    return act + branch + placed


def shards(
    tokens,
    cotangent,
    norm_gain,
    up_blocks,
    down_blocks,
    up_left,
    up_right,
    down_left,
    down_right,
    block_pattern,
    rank_used,
):
    sections = lax.axis_size("pipe")
    replicas = lax.axis_size("dp")
    section_index = lax.axis_index("pipe")
    last_section = sections - 1
    micro_rows = tokens.shape[0]
    feature_width = tokens.shape[1]
    section_params = (
        up_blocks[0],
        down_blocks[0],
        up_left[0],
        up_right[0],
        down_left[0],
        down_right[0],
        norm_gain[0],
    )
    section_pattern = block_pattern[0]
    section_ranks = rank_used[0]
    turns = 2 * sections - 1

    def mapped(act, params):
        return layer_apply(act, params, section_pattern, section_ranks)

    def forward_apply(source):
        return mapped(source.astype(jnp.float32), section_params).astype(jnp.bfloat16)

    def forward_spare(source):
        return jnp.zeros_like(source)

    forward_store = tokens
    backward_store = cotangent

    def place_result(handoff_store, emit_rows, result):
        return jnp.where(emit_rows, result, handoff_store)

    def forward_compute(step_index, incoming, handoff_store, saved_inputs):
        micro_index = step_index - section_index
        active = jnp.logical_and(micro_index >= 0, micro_index < sections)
        slot_index = jnp.clip(micro_index, 0, last_section)
        first_rows = handoff_store
        source = jnp.where(section_index == 0, first_rows, incoming)
        result = lax.cond(active, forward_apply, forward_spare, source)
        kept = lax.dynamic_index_in_dim(saved_inputs, slot_index, 0, keepdims=False)
        saved_inputs = lax.dynamic_update_index_in_dim(
            saved_inputs, jnp.where(active, source, kept), slot_index, 0
        )
        emit_rows = jnp.logical_and(active, section_index == last_section)
        handoff_store = place_result(handoff_store, emit_rows, result)
        return (result, handoff_store, saved_inputs)

    def forward_turn(step_index, loop_state):
        incoming, handoff_store, saved_inputs = loop_state
        result, handoff_store, saved_inputs = forward_compute(
            step_index, incoming, handoff_store, saved_inputs
        )
        incoming = from_behind(result, "pipe", 1)
        handoff_store = from_behind(handoff_store, "pipe", -1)
        return (incoming, handoff_store, saved_inputs)

    saved_start = jnp.zeros((sections, micro_rows, feature_width), jnp.bfloat16)
    zero_rows = jnp.zeros((micro_rows, feature_width), jnp.bfloat16)
    loop_state = lax.fori_loop(0, turns - 1, forward_turn, (zero_rows, forward_store, saved_start))
    unused, forward_store, saved_inputs = forward_compute(
        turns - 1, loop_state[0], loop_state[1], loop_state[2]
    )
    zero_grads = tuple((jnp.zeros_like(item) for item in section_params))

    def backward_apply(operands):
        source, upstream, totals = operands
        unused_out, pull = jax.vjp(mapped, source.astype(jnp.float32), section_params)
        act_grad, param_grads = pull(upstream.astype(jnp.float32))
        new_totals = tuple((old + new for old, new in zip(totals, param_grads)))
        return (act_grad.astype(jnp.bfloat16), new_totals)

    def backward_spare(operands):
        return (jnp.zeros_like(operands[0]), operands[2])

    def backward_compute(step_index, incoming, handoff_store, totals):
        micro_index = 2 * last_section - step_index - section_index
        active = jnp.logical_and(micro_index >= 0, micro_index < sections)
        slot_index = jnp.clip(micro_index, 0, last_section)
        top_rows = handoff_store
        upstream = jnp.where(section_index == last_section, top_rows, incoming)
        source = lax.dynamic_index_in_dim(saved_inputs, slot_index, 0, keepdims=False)
        result, totals = lax.cond(
            active, backward_apply, backward_spare, (source, upstream, totals)
        )
        emit_rows = jnp.logical_and(active, section_index == 0)
        handoff_store = place_result(handoff_store, emit_rows, result)
        return (result, handoff_store, totals)

    def backward_turn(step_index, loop_state):
        incoming, handoff_store, totals = loop_state
        result, handoff_store, totals = backward_compute(
            step_index, incoming, handoff_store, totals
        )
        incoming = from_behind(result, "pipe", -1)
        handoff_store = from_behind(handoff_store, "pipe", 1)
        return (incoming, handoff_store, totals)

    loop_state = lax.fori_loop(0, turns - 1, backward_turn, (zero_rows, backward_store, zero_grads))
    unused, backward_store, totals = backward_compute(
        turns - 1, loop_state[0], loop_state[1], loop_state[2]
    )
    expanded = tuple((item[None] for item in totals))
    summed = (
        lax.psum_scatter(expanded[0], "dp", scatter_dimension=3, tiled=True),
        lax.psum_scatter(expanded[1], "dp", scatter_dimension=3, tiled=True),
        lax.psum_scatter(expanded[2], "dp", scatter_dimension=2, tiled=True),
        lax.psum_scatter(expanded[3], "dp", scatter_dimension=2, tiled=True),
        lax.psum_scatter(expanded[4], "dp", scatter_dimension=2, tiled=True),
        lax.psum_scatter(expanded[5], "dp", scatter_dimension=2, tiled=True),
        lax.psum_scatter(expanded[6], "dp", scatter_dimension=1, tiled=True),
    )
    factor = 1.0 / math.sqrt(micro_rows * sections * replicas)
    scaled = [item * factor for item in summed]
    return (
        forward_store,
        backward_store,
        scaled[0],
        scaled[1],
        scaled[2],
        scaled[3],
        scaled[4],
        scaled[5],
        scaled[6],
    )


def solution(mesh):
    return jax.shard_map(
        shards,
        mesh=mesh,
        in_specs=(
            P(("pipe", "dp"), None),
            P(("pipe", "dp"), None),
            P("pipe", None),
            P("pipe", None, None, None),
            P("pipe", None, None, None),
            P("pipe", None, None),
            P("pipe", None, None),
            P("pipe", None, None),
            P("pipe", None, None),
            P("pipe", None, None, None),
            P("pipe", None),
        ),
        out_specs=(
            P(("pipe", "dp"), None),
            P(("pipe", "dp"), None),
            P("pipe", None, None, "dp"),
            P("pipe", None, None, "dp"),
            P("pipe", None, "dp"),
            P("pipe", None, "dp"),
            P("pipe", None, "dp"),
            P("pipe", None, "dp"),
            P("pipe", "dp"),
        ),
        check_vma=False,
    )
```

profile of v0, /device:TPU:0, one launch (start us, length us, event | category | flops | bytes accessed | tf_op | source)
XLA Modules:
  0.0 707.7 jit_solution(10713957491805530718)
XLA Ops:
  9.8 60.9 %while.48 = (s32[]{:T(128)}, bf16[16,6144]{1,0:T(8,128)(2,1)S(1)}, bf16[16,6144]{1,0:T(8,128)(2,1)S(1)}, bf16[2,16,6144]{2,1,0:T(8,128)(2,1)S(1)}, s32[]{:T(128)...) while((s32[]{:T(128)}, bf16[16,6144]{1,0:T(8,128)(2,1)S(1)}, ...), condition=%wide.region_4.5_spmd, body=%wide.region_0.4_spmd.sunk | while | flops 203295040 | bytes 28658800 | solution.py:143
  10.0 20.4 %conditional.8 = (bf16[16,6144]{1,0:T(8,128)(2,1)S(1)}) conditional(s32[]{:T(128)} %convert_element_type.134, () %tuple.129, (bf16[16,6144]{1,0:T(8,128)(2,1)S(1)}, f32[1,6144]{1,0:T(1,128)}, f32[8,6144]{1,0:T(8,128)}, s32[2]{0:T(128)}, f32[8,24576]{1,0:T(8,128)}, /*index=5*/s32[2,2,4]{2,1,0:T(2,128)}, f32[4,96,384]{2,1,0:T(8,128)}, ...), branch_computations={%region_1.1_spmd, %region_2.3_spmd} | conditional | flops 203000112 | bytes 25119448 | solution.py:123
  17.5 2.5 fusion.298
  20.3 2.0 fusion.5
  26.7 3.2 convolution_multiply_fusion
  31.7 4.6 collective-permute-start
  36.3 3.3 collective-permute-done.1
  40.9 20.4 %conditional.8 = (bf16[16,6144]{1,0:T(8,128)(2,1)S(1)}) conditional(s32[]{:T(128)} %convert_element_type.134, () %tuple.129, (bf16[16,6144]{1,0:T(8,128)(2,1)S(1)}, f32[1,6144]{1,0:T(1,128)}, f32[8,6144]{1,0:T(8,128)}, s32[2]{0:T(128)}, f32[8,24576]{1,0:T(8,128)}, /*index=5*/s32[2,2,4]{2,1,0:T(2,128)}, f32[4,96,384]{2,1,0:T(8,128)}, ...), branch_computations={%region_1.1_spmd, %region_2.3_spmd} | conditional | flops 203000112 | bytes 25119448 | solution.py:123
  48.4 2.5 fusion.298
  51.2 2.0 fusion.5
  57.6 3.2 convolution_multiply_fusion
  62.6 4.6 collective-permute-start
  67.2 2.4 collective-permute-done.1
  76.2 147.5 %while.49 = (s32[]{:T(128)}, bf16[16,6144]{1,0:T(8,128)(2,1)}, bf16[16,6144]{1,0:T(8,128)(2,1)}, f32[4,96,384]{2,1,0:T(8,128)S(1)}, f32[4,96,384]{2,1,0:T(8,128)...) while((s32[]{:T(128)}, bf16[16,6144]{1,0:T(8,128)(2,1)}, ...), condition=%wide.region_14.15_spmd, body=%wide.region_8.14_spmd.sunk | while | flops 521703584 | bytes 92838432 | solution.py:182
  78.2 60.7 %collective-permute-start.3 = (bf16[16,6144]{1,0:T(8,128)(2,1)S(1)}, bf16[16,6144]{1,0:T(8,128)(2,1)S(1)}, u32[]{:S(2)}, u32[]{:S(2)}) collective-permute-start(bf16[16,6144]{1,0:T(8,128)(2,1)S(1)} %broadcast_select_fusion.13), channel_id=1, source_target_pairs={{0,16},{1,17},{2,18},{3,19},{4,20},{5,21},{6,22},{7,23},{8,24},{9,... | collective-permute-start | bytes 589832 | tf_op jit(solution)/shard_map/while/body/eval_jaxpr/ppermute | solution.py:14
  140.2 1.9 collective-permute-done.3
  142.1 4.6 collective-permute-done.2
  147.3 57.0 %conditional.9 = (bf16[16,6144]{1,0:T(8,128)(2,1)}, f32[4,96,384]{2,1,0:T(8,128)S(1)}, f32[4,96,384]{2,1,0:T(8,128)S(1)}, f32[8,6144]{1,0:T(8,128)}, f32[8,24576...) conditional(s32[]{:T(128)} %convert_element_type.135, (f32[4,96,384]{2,1,0:T(8,128)S(1)}, ...), branch_computations={%region_9.9_spmd, %region_10.13_spmd} | conditional | flops 521605280 | bytes 89102248 | solution.py:166
  151.2 2.6 fusion.300
  159.7 3.1 add_multiply_fusion
  163.9 2.6 fusion.301
  169.1 4.6 fusion.100
  174.6 3.1 convolution_multiply_fusion.5
  182.6 2.1 reshape.224
  184.7 1.9 fusion.117
  196.3 2.9 convolution_add_fusion.2
  199.2 3.2 convolution_multiply_fusion.4
  202.5 1.8 convolution_add_fusion.5
  208.1 1.9 collective-permute-done.3
  210.0 4.6 collective-permute-done.2
  223.8 55.9 %conditional.5 = (bf16[16,6144]{1,0:T(8,128)(2,1)}, f32[4,96,384]{2,1,0:T(8,128)S(1)}, f32[4,96,384]{2,1,0:T(8,128)S(1)}, f32[8,6144]{1,0:T(8,128)}, f32[8,24576...) conditional(s32[]{:T(128)} %convert_element_type.79, ...), branch_computations={%region_15.16_spmd, %region_16.20_spmd} | conditional | flops 521605280 | bytes 107975688 | solution.py:166
  227.6 2.6 fusion.302
  236.9 3.7 add_multiply_fusion.1
  241.6 2.6 fusion.303
  246.7 4.1 fusion.198
  251.8 3.3 convolution_multiply_fusion.9
  256.0 1.8 fusion.229
  271.5 2.9 convolution_add_fusion.9
  274.4 3.2 convolution_multiply_fusion.8
  277.6 1.8 convolution_add_fusion.12
  279.7 2.9 copy.52
  290.9 59.0 %reduce-scatter.22.cloned.1.call-done = f32[384,1]{1,0:T(8,128)} async-done(((f32[6144,1]{1,0:T(8,128)}), f32[384,1]{1,0:T(8,128)}) %reduce-scatter.22.cloned.1.call-update) | async-done | bytes 1552
  351.5 54.5 %reduce-scatter.20.cloned.1.call-done = f32[1,8,384]{2,1,0:T(8,128)} async-done(((f32[1,8,6144]{2,1,0:T(8,128)}), f32[1,8,384]{2,1,0:T(8,128)}) %reduce-scatter.20.cloned.1.call-update) | async-done | bytes 12304 | tf_op jit(solution)/shard_map/reduce_scatter | solution.py:193
  407.3 54.9 %reduce-scatter.14.cloned.1.call-done = f32[1,8,384]{2,1,0:T(8,128)} async-done(((f32[1,8,6144]{2,1,0:T(8,128)}), f32[1,8,384]{2,1,0:T(8,128)}) %reduce-scatter.14.cloned.1.call-update) | async-done | bytes 12304 | tf_op jit(solution)/shard_map/reduce_scatter | solution.py:190
  463.5 57.6 %reduce-scatter.12.cloned.1.call-done = f32[1,4,96,24]{2,3,1,0:T(8,128)} async-done(((f32[1,4,96,384]{2,3,1,0:T(8,128)}), f32[1,4,96,24]{2,3,1,0:T(8,128)}) %reduce-scatter.12.cloned.1.call-update) | async-done | bytes 36880 | tf_op jit(solution)/shard_map/reduce_scatter | solution.py:189
  522.5 58.0 %reduce-scatter.10.cloned.1.call-done = f32[1,4,96,24]{2,3,1,0:T(8,128)} async-done(((f32[1,4,96,384]{2,3,1,0:T(8,128)}), f32[1,4,96,24]{2,3,1,0:T(8,128)}) %reduce-scatter.10.cloned.1.call-update) | async-done | bytes 36880 | tf_op jit(solution)/shard_map/reduce_scatter | solution.py:188
  581.9 57.6 %reduce-scatter.18.cloned.1.call-done = f32[1,8,1536]{2,1,0:T(8,128)} async-done(((f32[1,8,24576]{2,1,0:T(8,128)}), f32[1,8,1536]{2,1,0:T(8,128)}) %reduce-scatter.18.cloned.1.call-update) | async-done | bytes 49168 | tf_op jit(solution)/shard_map/reduce_scatter | solution.py:192
  640.9 58.1 %reduce-scatter.16.cloned.1.call-done = f32[1,8,1536]{2,1,0:T(8,128)} async-done(((f32[1,8,24576]{2,1,0:T(8,128)}), f32[1,8,1536]{2,1,0:T(8,128)}) %reduce-scatter.16.cloned.1.call-update) | async-done | bytes 49168 | tf_op jit(solution)/shard_map/reduce_scatter | solution.py:191
  (333 shorter events, 123.0 us)
Async XLA Ops:
  7.2 342.7 %reduce-scatter.22.cloned.1.call-start = ((), (), s32[]{:S(2)}) async-start(), calls=%async_computation.13 | async-start | bytes 3342336
  26.0 3.9 copy-start.36
  30.4 9.2 %collective-permute-start.1 = (bf16[16,6144]{1,0:T(8,128)(2,1)S(1)}, bf16[16,6144]{1,0:T(8,128)(2,1)S(1)}, u32[]{:S(2)}, u32[]{:S(2)}) collective-permute-start(bf16[16,6144]{1,0:T(8,128)(2,1)S(1)} %broadcast_select_fusion.12), channel_id=1, source_target_pairs={{16,0},{17,1},{18,2},{19,3},{20,4},{21,5},{22,6},{23,7},{24,8},{25... | collective-permute-start | bytes 589832 | tf_op jit(solution)/shard_map/while/body/eval_jaxpr/ppermute | solution.py:14
  31.7 9.0 %collective-permute-start = (bf16[16,6144]{1,0:T(8,128)(2,1)S(1)}, bf16[16,6144]{1,0:T(8,128)(2,1)S(1)}, u32[]{:S(2)}, u32[]{:S(2)}) collective-permute-start(bf16[16,6144]{1,0:T(8,128)(2,1)S(1)} %get-tuple-element.1686), channel_id=1, source_target_pairs={{0,16},{1,17},{2,18},{3,19},{4,20},{5,21},{6,22},{7,23},{8,24},{9,... | collective-permute-start | bytes 589832 | tf_op jit(solution)/shard_map/while/body/eval_jaxpr/ppermute | solution.py:14
  56.9 3.9 copy-start.36
  61.3 8.2 %collective-permute-start.1 = (bf16[16,6144]{1,0:T(8,128)(2,1)S(1)}, bf16[16,6144]{1,0:T(8,128)(2,1)S(1)}, u32[]{:S(2)}, u32[]{:S(2)}) collective-permute-start(bf16[16,6144]{1,0:T(8,128)(2,1)S(1)} %broadcast_select_fusion.12), channel_id=1, source_target_pairs={{16,0},{17,1},{18,2},{19,3},{20,4},{21,5},{22,6},{23,7},{24,8},{25... | collective-permute-start | bytes 589832 | tf_op jit(solution)/shard_map/while/body/eval_jaxpr/ppermute | solution.py:14
  62.6 8.1 %collective-permute-start = (bf16[16,6144]{1,0:T(8,128)(2,1)S(1)}, bf16[16,6144]{1,0:T(8,128)(2,1)S(1)}, u32[]{:S(2)}, u32[]{:S(2)}) collective-permute-start(bf16[16,6144]{1,0:T(8,128)(2,1)S(1)} %get-tuple-element.1686), channel_id=1, source_target_pairs={{0,16},{1,17},{2,18},{3,19},{4,20},{5,21},{6,22},{7,23},{8,24},{9,... | collective-permute-start | bytes 589832 | tf_op jit(solution)/shard_map/while/body/eval_jaxpr/ppermute | solution.py:14
  78.2 63.9 %collective-permute-start.3 = (bf16[16,6144]{1,0:T(8,128)(2,1)S(1)}, bf16[16,6144]{1,0:T(8,128)(2,1)S(1)}, u32[]{:S(2)}, u32[]{:S(2)}) collective-permute-start(bf16[16,6144]{1,0:T(8,128)(2,1)S(1)} %broadcast_select_fusion.13), channel_id=1, source_target_pairs={{0,16},{1,17},{2,18},{3,19},{4,20},{5,21},{6,22},{7,23},{8,24},{9,... | collective-permute-start | bytes 589832 | tf_op jit(solution)/shard_map/while/body/eval_jaxpr/ppermute | solution.py:14
  138.9 7.8 %collective-permute-start.2 = (bf16[16,6144]{1,0:T(8,128)(2,1)}, bf16[16,6144]{1,0:T(8,128)(2,1)S(1)}, u32[]{:S(2)}, u32[]{:S(2)}) collective-permute-start(bf16[16,6144]{1,0:T(8,128)(2,1)} %get-tuple-element.1510), channel_id=1, source_target_pairs={{16,0},{17,1},{18,2},{19,3},{20,4},{21,5},{22,6},{23,7},{24,8},{25... | collective-permute-start | bytes 589832 | tf_op jit(solution)/shard_map/while/body/eval_jaxpr/ppermute | solution.py:14
  142.1 4.6 copy-start.31
  147.3 6.4 copy-start.10
  147.3 6.4 copy-start.20
  147.5 6.5 copy-start.76
  149.6 4.5 copy-start.74
  155.6 7.3 %copy-start.65 = (s32[4]{0:T(128)}, s32[4]{0:T(128)S(1)}, u32[]{:S(2)}) copy-start(s32[4]{0:T(128)S(1)} %get-tuple-element.1244) | copy-start | bytes 52 | tf_op jit(solution)/shard_map/while/body/eval_jaxpr/cond
  155.6 7.3 %copy-start.67 = (s32[4]{0:T(128)}, s32[4]{0:T(128)S(1)}, u32[]{:S(2)}) copy-start(s32[4]{0:T(128)S(1)} %get-tuple-element.1245) | copy-start | bytes 52 | tf_op jit(solution)/shard_map/while/body/eval_jaxpr/cond
  159.7 3.2 copy-start.30
  159.7 3.9 copy-start.37
  162.9 5.1 copy-start
  168.6 5.1 copy-start.52
  177.7 3.4 copy-start.66
  184.7 5.8 copy-start.6
  199.2 3.2 copy-start.1
  199.2 5.1 copy-start.13
  199.2 5.1 copy-start.23
  205.3 4.7 collective-permute-start.3
  206.8 7.8 %collective-permute-start.2 = (bf16[16,6144]{1,0:T(8,128)(2,1)}, bf16[16,6144]{1,0:T(8,128)(2,1)S(1)}, u32[]{:S(2)}, u32[]{:S(2)}) collective-permute-start(bf16[16,6144]{1,0:T(8,128)(2,1)} %get-tuple-element.1510), channel_id=1, source_target_pairs={{16,0},{17,1},{18,2},{19,3},{20,4},{21,5},{22,6},{23,7},{24,8},{25... | collective-permute-start | bytes 589832 | tf_op jit(solution)/shard_map/while/body/eval_jaxpr/ppermute | solution.py:14
  210.0 4.6 copy-start.31
  223.8 7.9 %copy-start.14 = (f32[4,96,384]{2,1,0:T(8,128)}, f32[4,96,384]{2,1,0:T(8,128)S(1)}, u32[]{:S(2)}) copy-start(f32[4,96,384]{2,1,0:T(8,128)S(1)} %get-tuple-element.1088) | copy-start | bytes 1769476 | tf_op jit(solution)/shard_map/cond
  223.8 7.8 %copy-start.24 = (f32[4,96,384]{2,1,0:T(8,128)}, f32[4,96,384]{2,1,0:T(8,128)S(1)}, u32[]{:S(2)}) copy-start(f32[4,96,384]{2,1,0:T(8,128)S(1)} %get-tuple-element.1089) | copy-start | bytes 1769476 | tf_op jit(solution)/shard_map/cond
  231.7 5.1 copy-start.54
  232.8 14.0 %copy-start.77 = (s32[4]{0:T(128)}, s32[4]{0:T(128)S(1)}, u32[]{:S(2)}) copy-start(s32[4]{0:T(128)S(1)} %get-tuple-element.1251) | copy-start | bytes 52 | tf_op jit(solution)/shard_map/cond
  236.8 3.7 copy-start.33
  236.9 3.7 copy-start.49
  236.9 4.4 copy-start.39
  240.6 21.9 %copy-start.55 = (bf16[16,6144]{1,0:T(8,128)(2,1)}, bf16[16,6144]{1,0:T(8,128)(2,1)S(1)}, u32[]{:S(2)}) copy-start(bf16[16,6144]{1,0:T(8,128)(2,1)S(1)} %broadcast_select_fusion.4) | copy-start | bytes 589828 | tf_op jit(solution)/shard_map/cond
  241.3 4.4 copy-start.79
  246.2 4.6 copy-start.63
  259.4 6.1 copy-start.8
  274.4 3.2 copy-start.56
  274.4 5.1 copy-start.17
  274.4 5.1 copy-start.27
  282.7 123.3 %reduce-scatter.20.cloned.1.call-start = ((), (), s32[]{:S(2)}) async-start(), calls=%async_computation.12 | async-start | bytes 208896 | tf_op jit(solution)/shard_map/reduce_scatter | solution.py:193
  283.4 178.7 %reduce-scatter.14.cloned.1.call-start = ((), (), s32[]{:S(2)}) async-start(), calls=%async_computation.9 | async-start | bytes 208896 | tf_op jit(solution)/shard_map/reduce_scatter | solution.py:190
  284.2 236.9 %reduce-scatter.12.cloned.1.call-start = ((), (), s32[]{:S(2)}) async-start(), calls=%async_computation.8 | async-start | bytes 835584 | tf_op jit(solution)/shard_map/reduce_scatter | solution.py:189
  285.4 295.1 %reduce-scatter.10.cloned.1.call-start = ((), (), s32[]{:S(2)}) async-start(), calls=%async_computation.7 | async-start | bytes 835584 | tf_op jit(solution)/shard_map/reduce_scatter | solution.py:188
  286.7 352.7 %reduce-scatter.18.cloned.1.call-start = ((), (), s32[]{:S(2)}) async-start(), calls=%async_computation.11 | async-start | bytes 835584 | tf_op jit(solution)/shard_map/reduce_scatter | solution.py:192
  287.3 411.6 %reduce-scatter.16.cloned.1.call-start = ((), (), s32[]{:S(2)}) async-start(), calls=%async_computation.10 | async-start | bytes 835584 | tf_op jit(solution)/shard_map/reduce_scatter | solution.py:191
  (52 other events, 108.0 us)
Sparse Core Ops, SparseCore 0:
  282.8 67.0 reduce-scatter.21
  353.4 52.5 reduce-scatter.19
  409.5 52.6 reduce-scatter.13
  465.6 55.4 reduce-scatter.11
  524.9 55.5 reduce-scatter.9
  583.9 55.5 reduce-scatter.17
  643.4 55.4 reduce-scatter.15
where the time goes:
time: 718 us; the launch traced here: 708 us
  waiting for transfers between devices  423 us (59%)
  matrix products  107 us (15%)
  starting transfers between devices  76.8 us (11%)
  local copies, waits for them, and re-layouts  44.4 us (6%)
  other arithmetic  31 us (4%)
  between operations  14.8 us (2%)
  loops' own time  10.5 us (1%)
    ppermute x8, starting transfers between devices, from_behind(): return lax.ppermute(block, axis, route)  76.5 us
    unnamed x8, waiting for transfers between devices  61.6 us
    reduce_scatter x1, waiting for transfers between devices, shards(): lax.psum_scatter(expanded[3], 'dp', scatter_dimension=2, tiled=True)  58.1 us
    reduce_scatter x1, waiting for transfers between devices, shards(): lax.psum_scatter(expanded[0], 'dp', scatter_dimension=3, tiled=True)  58 us
    reduce_scatter x1, waiting for transfers between devices, shards(): lax.psum_scatter(expanded[1], 'dp', scatter_dimension=3, tiled=True)  57.6 us
    reduce_scatter x1, waiting for transfers between devices, shards(): lax.psum_scatter(expanded[4], 'dp', scatter_dimension=2, tiled=True)  57.6 us
    reduce_scatter x1, waiting for transfers between devices, shards(): lax.psum_scatter(expanded[2], 'dp', scatter_dimension=2, tiled=True)  54.9 us
    reduce_scatter x1, waiting for transfers between devices, shards(): lax.psum_scatter(expanded[5], 'dp', scatter_dimension=2, tiled=True)  54.5 us
  transfers between devices with their start and end apart: 15, of which 15 were waited for; matrix products, arithmetic and copies ran while one was open for 2% of the time, Pallas kernels for 0%

commit v1 on v0

--- a/solution.py
+++ b/solution.py
@@ -208,9 +208,210 @@
     )
 
 
+def matmul(a, b, ca, cb):
+    return lax.dot_general(
+        a, b, (((ca,), (cb,)), ((), ())),
+        precision=lax.Precision.HIGH, preferred_element_type=jnp.float32,
+    )
+
+
+def take_block(rows, index, width):
+    return lax.dynamic_slice_in_dim(rows, index * width, width, 1)
+
+
+def add_block(rows, part, index):
+    width = part.shape[1]
+    old = lax.dynamic_slice_in_dim(rows, index * width, width, 1)
+    return lax.dynamic_update_slice_in_dim(rows, old + part, index * width, 1)
+
+
+def masks(ranks, count):
+    rank_index = jnp.arange(count, dtype=jnp.int32)
+    return (
+        jnp.where(rank_index < ranks[0], 1.0, 0.0).astype(jnp.float32),
+        jnp.where(rank_index < ranks[1], 1.0, 0.0).astype(jnp.float32),
+    )
+
+
+def forward_pass(rows, params, pattern, ranks):
+    up_blocks, down_blocks, up_left, up_right, down_left, down_right, gain = params
+    act = rows.astype(jnp.float32)
+    blocks, feat, hid = up_blocks.shape
+    up_mask, down_mask = masks(ranks, up_left.shape[0])
+    scale = lax.rsqrt(jnp.mean(act * act, axis=1, keepdims=True) + 1e-05)
+    normed = act * scale * gain
+    low = matmul(normed, up_left, 1, 1) * up_mask
+    pre = matmul(low, up_right, 1, 0)
+    for k in range(blocks):
+        part = matmul(take_block(normed, pattern[0, 0, k], feat), up_blocks[k], 1, 0)
+        pre = add_block(pre, part, pattern[0, 1, k])
+    hidden = gelu_tanh(pre)
+    low_down = matmul(hidden, down_left, 1, 1) * down_mask
+    out = act + matmul(low_down, down_right, 1, 0)
+    for k in range(blocks):
+        part = matmul(take_block(hidden, pattern[1, 0, k], hid), down_blocks[k], 1, 1)
+        out = add_block(out, part, pattern[1, 1, k])
+    return out.astype(jnp.bfloat16), (scale, low, pre, low_down)
+
+
+def backward_pass(rows, upstream, saved, params, pattern, ranks, replicas):
+    up_blocks, down_blocks, up_left, up_right, down_left, down_right, gain = params
+    scale, low, pre, low_down = saved
+    act = rows.astype(jnp.float32)
+    grad = upstream.astype(jnp.float32)
+    blocks, feat, hid = up_blocks.shape
+    up_mask, down_mask = masks(ranks, up_left.shape[0])
+    unit = act * scale
+    normed = unit * gain
+    tanh = jnp.tanh(0.7978845608028654 * (pre + 0.044715 * pre * pre * pre))
+    hidden = 0.5 * pre * (1.0 + tanh)
+    slope = 0.5 * (1.0 + tanh) + 0.5 * pre * (1.0 - tanh * tanh) * (
+        0.7978845608028654 * (1.0 + 3.0 * 0.044715 * pre * pre)
+    )
+    d_low_down = matmul(grad, down_right, 1, 1) * down_mask
+    d_hidden = matmul(d_low_down, down_left, 1, 0)
+    g_down = []
+    for k in range(blocks):
+        piece = take_block(grad, pattern[1, 1, k], feat)
+        d_hidden = add_block(d_hidden, matmul(piece, down_blocks[k], 1, 0), pattern[1, 0, k])
+        g_down.append(matmul(take_block(hidden, pattern[1, 0, k], hid), piece, 0, 0))
+    d_pre = d_hidden * slope
+    d_low = matmul(d_pre, up_right, 1, 1) * up_mask
+    d_normed = matmul(d_low, up_left, 1, 0)
+    g_up = []
+    for k in range(blocks):
+        piece = take_block(d_pre, pattern[0, 1, k], hid)
+        d_normed = add_block(d_normed, matmul(piece, up_blocks[k], 1, 1), pattern[0, 0, k])
+        g_up.append(matmul(piece, take_block(normed, pattern[0, 0, k], feat), 0, 0))
+    scaled = d_normed * gain
+    act_grad = grad + scale * (scaled - unit * jnp.mean(scaled * unit, axis=1, keepdims=True))
+    g_gain = jnp.sum(d_normed * unit, axis=0)
+
+    def by_share(g):
+        return g.reshape(g.shape[0], replicas, -1).transpose(1, 0, 2)
+
+    def block_share(g):
+        whole = jnp.concatenate(g, axis=1)
+        eighths = whole.reshape(replicas, -1, 8, whole.shape[1]).transpose(0, 2, 1, 3)
+        return eighths.reshape(replicas, 8, -1)
+
+    gain_rows = jnp.pad(g_gain.reshape(replicas, 1, -1), ((0, 0), (0, 7), (0, 0)))
+    packed = jnp.concatenate(
+        [
+            by_share(matmul(low, d_pre, 0, 0)),
+            by_share(matmul(d_low_down, hidden, 0, 0)),
+            by_share(matmul(d_low, normed, 0, 0)),
+            by_share(matmul(low_down, grad, 0, 0)),
+            block_share(g_up),
+            block_share(g_down),
+            gain_rows,
+        ],
+        axis=2,
+    )
+    return act_grad.astype(jnp.bfloat16), packed
+
+
+def reduce_shares(packed):
+    return lax.psum_scatter(packed, "dp", scatter_dimension=0, tiled=False)
+
+
+def two_sections(
+    tokens,
+    cotangent,
+    norm_gain,
+    up_blocks,
+    down_blocks,
+    up_left,
+    up_right,
+    down_left,
+    down_right,
+    block_pattern,
+    rank_used,
+):
+    replicas = lax.axis_size("dp")
+    section = lax.axis_index("pipe")
+    count, width = tokens.shape
+    params = (
+        up_blocks[0],
+        down_blocks[0],
+        up_left[0],
+        up_right[0],
+        down_left[0],
+        down_right[0],
+        norm_gain[0],
+    )
+    pattern = block_pattern[0]
+    ranks = rank_used[0]
+    forth, back = [(0, 1)], [(1, 0)]
+    first = jnp.concatenate([tokens, lax.ppermute(tokens, "pipe", back)], axis=0)
+    top = jnp.concatenate([lax.ppermute(cotangent, "pipe", forth), cotangent], axis=0)
+
+    def run(rows):
+        return forward_pass(rows, params, pattern, ranks)
+
+    def skip_forward(rows):
+        return jax.tree.map(lambda t: jnp.zeros(t.shape, t.dtype), jax.eval_shape(run, rows))
+
+    result, saved = lax.cond(section == 0, run, skip_forward, first)
+    second = lax.ppermute(result, "pipe", forth)
+
+    def last(operands):
+        rows, upstream = operands
+        out, kept = run(rows)
+        below, packed = backward_pass(rows, upstream, kept, params, pattern, ranks, replicas)
+        return out, below, packed
+
+    def skip_last(operands):
+        return jax.tree.map(lambda t: jnp.zeros(t.shape, t.dtype), jax.eval_shape(last, operands))
+
+    final, below, packed = lax.cond(section == 1, last, skip_last, (second, top))
+    from_above = lax.ppermute(below, "pipe", back)
+    final_early = lax.ppermute(final[:count], "pipe", back)
+
+    def first_back(operands):
+        upstream, kept, unused = operands
+        return backward_pass(first, upstream, kept, params, pattern, ranks, replicas)
+
+    def skip_back(operands):
+        return operands[0], operands[2]
+
+    bottom, packed = lax.cond(section == 0, first_back, skip_back, (from_above, saved, packed))
+    bottom_late = lax.ppermute(bottom[count:], "pipe", forth)
+    final_tokens = jnp.where(section == 0, final_early, final[count:])
+    input_gradient = jnp.where(section == 0, bottom[:count], bottom_late)
+    factor = 1.0 / math.sqrt(count * 2 * replicas)
+    share = reduce_shares(packed) * factor
+    blocks, feat, hid = params[0].shape
+    hidden_share = params[3].shape[1] // replicas
+    width_share = width // replicas
+    block_columns = hid // replicas // 8 * blocks * feat
+    pieces = []
+    start = 0
+    for extent in (hidden_share, hidden_share, width_share, width_share, block_columns, block_columns, width_share):
+        pieces.append(share[:, start : start + extent])
+        start += extent
+
+    def unpack(piece):
+        rows = piece.reshape(8, -1, blocks * feat).transpose(1, 0, 2).reshape(-1, blocks, feat)
+        return rows.transpose(1, 2, 0)[None]
+
+    return (
+        final_tokens,
+        input_gradient,
+        unpack(pieces[4]),
+        unpack(pieces[5]),
+        pieces[2][None],
+        pieces[0][None],
+        pieces[1][None],
+        pieces[3][None],
+        pieces[6][:1],
+    )
+
+
 def solution(mesh):
+    body = two_sections if mesh.shape["pipe"] == 2 and mesh.shape["dp"] == 16 else shards
     return jax.shard_map(
-        shards,
+        body,
         mesh=mesh,
         in_specs=(
             P(("pipe", "dp"), None),

time: 718 us -> 315 us (0.44); the launches traced: 708 us -> 313 us
  waiting for transfers between devices: 423 us -> 165 us
  starting transfers between devices: 76.8 us -> 15.3 us
  matrix products: 107 us -> 45.7 us
  other arithmetic: 31 us -> 18.8 us
  local copies, waits for them, and re-layouts: 44.4 us -> 33.1 us
  loops' own time: 10.5 us -> 20.8 us
    reduce_scatter x6 -> x0, waiting for transfers between devices: 341 us -> none  [the longest x1 58.1 us: shards(): lax.psum_scatter(expanded[3], 'dp', scatter_dimension=2, tiled=True)]
    ppermute x8 -> x6, waiting for transfers between devices: 21 us -> 107 us  [the longest x1 96.2 us: two_sections(): from_above = lax.ppermute(below, 'pipe', back)]
    dot_general x66 -> x36, matrix products: 107 us -> 45.7 us  [matmul(): lax.dot_general(a, b, (((ca,), (cb,)), ((), ())), precision=lax.Precision...]
    ppermute x8 -> x6, starting transfers between devices: 76.5 us -> 15.3 us  [the longest x1 5.53 us: two_sections(): lax.ppermute(cotangent, 'pipe', forth)]
    another operation x8 -> x3, loops' own time: 10.5 us -> 20.8 us  [the longest x1 10.4 us: two_sections(): result, saved = lax.cond(section == 0, run, skip_forward, first)]
    dynamic_update_slice x0 -> x8, local copies, waits for them, and re-layouts: none -> 7.67 us  [add_block(): return lax.dynamic_update_slice_in_dim(rows, old + part, index * width, 1)]
    cond x156 -> x42, local copies, waits for them, and re-layouts: 14.6 us -> 9 us
    unnamed x8 -> x2, waiting for transfers between devices: 61.6 us -> 57.7 us
  transfers between devices with their start and end apart: 15 -> 7, of which waited for: 15 -> 6; matrix products, arithmetic and copies ran while one was open for 2% -> 11% of each run, Pallas kernels for 0% -> 0%
where the time goes in v1:
time: 315 us; the launch traced here: 313 us
  waiting for transfers between devices  165 us (52%)
  matrix products  45.7 us (15%)
  local copies, waits for them, and re-layouts  33.1 us (11%)
  loops' own time  20.8 us (7%)
  other arithmetic  18.8 us (6%)
  starting transfers between devices  15.3 us (5%)
  between operations  14.2 us (5%)
    ppermute x1, waiting for transfers between devices, two_sections(): from_above = lax.ppermute(below, 'pipe', back)  96.2 us
    unnamed x2, waiting for transfers between devices  57.7 us
    dot_general x36, matrix products, matmul(): lax.dot_general(a, b, (((ca,), (cb,)), ((), ())), precision=lax.Precision...  45.7 us
    another operation x1, loops' own time, two_sections(): result, saved = lax.cond(section == 0, run, skip_forward, first)  10.4 us
    another operation x1, loops' own time, two_sections(): lax.cond(section == 0, first_back, skip_back, (from_above, saved, packed))  10.4 us
    cond x42, local copies, waits for them, and re-layouts  9 us
    dynamic_update_slice x8, local copies, waits for them, and re-layouts, add_block(): return lax.dynamic_update_slice_in_dim(rows, old + part, index * width, 1)  7.67 us
    ppermute x1, waiting for transfers between devices, two_sections(): second = lax.ppermute(result, 'pipe', forth)  7.12 us
  transfers between devices with their start and end apart: 7, of which 6 were waited for; matrix products, arithmetic and copies ran while one was open for 11% of the time, Pallas kernels for 0%

profile of v1, /device:TPU:0, one launch (start us, length us, event | category | flops | bytes accessed | tf_op | source)
XLA Modules:
  0.0 313.0 jit_solution(2952539343562625686)
XLA Ops:
  7.2 1.3 collective-permute-start
  8.5 5.5 %collective-permute-start.2 = (bf16[16,6144]{1,0:T(8,128)(2,1)}, bf16[16,6144]{1,0:T(8,128)(2,1)}, u32[]{:S(2)}, u32[]{:S(2)}) collective-permute-start(bf16[16,6144]{1,0:T(8,128)(2,1)} %param.18), channel_id=1, source_target_pairs={{0,16},{1,17},{2,18},{3,19},{4,20},{5,21},{6,22},{7,23},{8,24},{9,... | collective-permute-start | bytes 589832 | tf_op jit(solution)/shard_map/ppermute | solution.py:347
  15.0 1.6 collective-permute-done
  16.6 43.5 %conditional.3 = (bf16[32,6144]{1,0:T(8,128)(2,1)S(1)}, f32[32,1]{0,1:T(1,128)S(1)}, f32[32,8]{0,1:T(8,128)}, f32[32,24576]{1,0:T(8,128)}, f32[32,8]{0,1:T(8,128)}) conditional(s32[]{:T(128)} %convert_element_type.39, () %tuple.32, (bf16[32,6144]{1,0:T(8,128)(2,1)S(1)}, f32[1,6144]{1,0:T(1,128)}, f32[8,6144]{1,0:T(8,128)}, s32[2]{0:T(128)}, ...), branch_computations={%region_0.0_spmd, %region_1.3_spmd} | conditional | flops 165999168 | bytes 42215432 | solution.py:355
  16.9 1.3 fusion.225
  19.5 1.5 convolution_multiply_fusion.1
  21.0 1.7 fusion.224
  33.9 4.2 %fusion.231 = f32[32,24576]{1,0:T(8,128)} fusion(f32[32,8]{0,1:T(8,128)S(1)} %convolution_multiply_fusion.1, f32[8,24576]{1,0:T(8,128)} %get-tuple-element.80), kind=kOutput, calls=%fused_computation.329 | convolution fusion | flops 37748736 | bytes 3933184 | tf_op jit(solution)/shard_map/cond/branch_1_fun/dot_general | solution.py:212
  38.1 1.6 fusion.7
  39.7 1.6 fusion.6
  41.4 1.7 fusion.5
  43.0 1.7 fusion.4
  44.7 4.7 %convolution_multiply_fusion = f32[32,8]{0,1:T(8,128)} fusion(f32[8,24576]{1,0:T(8,128)S(1)} %copy-done.13, f32[8]{0:T(128)S(1)} %compare_select_fusion, f32[32,24576]{1,0:T(8,128)} %fusion.4), kind=kOutput, calls=%fused_computation.20 | convolution fusion | flops 44040448 | bytes 3933216 | tf_op jit(solution)/shard_map/cond/branch_1_fun/dot_general | solution.py:212
  49.3 1.2 convolution_add_fusion
  50.6 2.9 fusion.3
  53.4 1.6 copy-done.19
  60.1 1.3 collective-permute-start.1
  62.4 7.1 %collective-permute-done.1 = bf16[32,6144]{1,0:T(8,128)(2,1)S(1)} collective-permute-done((bf16[32,6144]{1,0:T(8,128)(2,1)S(1)}, bf16[32,6144]{1,0:T(8,128)(2,1)S(1)}, u32[]{:S(2)}, u32[]{:S(2)}) %collective-permute-start.1) | collective-permute-done | bytes 393248 | tf_op jit(solution)/shard_map/ppermute | solution.py:356
  69.6 2.0 conditional.4
  69.6 1.9 broadcast.181
  71.5 1.3 collective-permute-start.4
  72.8 96.2 %collective-permute-done.4 = bf16[32,6144]{1,0:T(8,128)(2,1)S(1)} collective-permute-done((bf16[32,6144]{1,0:T(8,128)(2,1)S(1)}, bf16[32,6144]{1,0:T(8,128)(2,1)S(1)}, u32[]{:S(2)}, u32[]{:S(2)}) %collective-permute-start.4) | collective-permute-done | bytes 393248 | tf_op jit(solution)/shard_map/ppermute | solution.py:368
  169.0 64.4 %conditional.5 = ((bf16[32,6144]{1,0:T(8,128)(2,1)S(1)}, f32[16,8,6528]{2,1,0:T(8,128)})) conditional(s32[]{:T(128)} %convert_element_type.39, (bf16[32,6144]{1,0:T(8,128)(2,1)S(1)}, f32[16,8,6528]{2,1,0:T(8,128)}) %tuple.35, (bf16[32,6144]{1,0:T(8,128)(2,1)S(1)}, f32[32,1]{0,1:T(1,128)}, f32[8,6144]{1,0:T(8,128)}, s32[2]{0:T(128)}, ...), branch_computations={%region_8.9_spmd, %region_9.12_spmd} | conditional | flops 321804832 | bytes 69000032 | solution.py:378
  169.0 1.4 fusion.229
  171.8 1.2 convolution_multiply_fusion.7
  173.0 1.7 fusion.228
  184.8 1.6 fusion.242
  186.4 2.6 fusion.238
  189.9 3.6 %multiply_multiply_fusion.2 = (f32[32,24576]{1,0:T(8,128)S(1)}, f32[32,24576]{1,0:T(8,128)S(1)}) fusion(f32[32,24576]{1,0:T(8,128)} %get-tuple-element.104, f32[32,24576]{1,0:T(8,128)S(1)} %fusion.165), kind=kLoop, calls=%fused_computation.223 | loop fusion | flops 14942208 | bytes 12582912 | tf_op jit(solution)/shard_map/cond/branch_1_fun/mul | solution.py:267
  193.5 1.4 convolution_multiply_fusion.6
  199.0 1.9 fusion.241
  201.9 2.2 copy.33
  204.1 1.8 fusion.222
  205.9 1.4 fusion.239
  209.4 1.4 dynamic_update_slice.92
  210.8 1.1 convolution_add_fusion.32
  211.9 1.4 dynamic_update_slice.93
  213.3 1.1 convolution_add_fusion.31
  214.4 1.5 dynamic_update_slice.94
  217.0 1.5 dynamic_update_slice.95
  218.5 2.0 multiply_reduce_fusion
  220.6 2.3 fusion.169
  224.3 1.8 fusion.240
  226.4 2.3 constant_dynamic-update-slice_fusion.11
  234.5 1.3 collective-permute-start.3
  235.8 4.6 %collective-permute-start.5 = (bf16[16,6144]{1,0:T(8,128)(2,1)S(1)}, bf16[16,6144]{1,0:T(8,128)(2,1)S(1)}, u32[]{:S(2)}, u32[]{:S(2)}) collective-permute-start(bf16[16,6144]{1,0:T(8,128)(2,1)S(1)} %slice.314), channel_id=1, source_target_pairs={{0,16},{1,17},{2,18},{3,19},{4,20},{5,21},{6,22},{7,23},{8,24},{9,... | collective-permute-start | bytes 589832 | tf_op jit(solution)/shard_map/ppermute | solution.py:379
  240.4 1.7 collective-permute-done.3
  244.3 57.7 %reduce-scatter.4.cloned.1.call-done = f32[1,8,6528]{2,1,0:T(8,128)} async-done(((f32[16,8,6528]{2,1,0:T(8,128)}), f32[1,8,6528]{2,1,0:T(8,128)}) %reduce-scatter.4.cloned.1.call-update) | async-done | bytes 208912
  (105 shorter events, 33.7 us)
Async XLA Ops:
  7.2 294.8 %reduce-scatter.4.cloned.1.call-start = ((), (), s32[]{:S(2)}) async-start(), calls=%async_computation.1 | async-start | bytes 3551232
  7.2 9.4 %collective-permute-start = (bf16[16,6144]{1,0:T(8,128)(2,1)}, bf16[16,6144]{1,0:T(8,128)(2,1)S(1)}, u32[]{:S(2)}, u32[]{:S(2)}) collective-permute-start(bf16[16,6144]{1,0:T(8,128)(2,1)} %param.17), channel_id=1, source_target_pairs={{16,0},{17,1},{18,2},{19,3},{20,4},{21,5},{22,6},{23,7},{24,8},{25... | collective-permute-start | bytes 589832 | tf_op jit(solution)/shard_map/ppermute | solution.py:346
  8.5 52.9 %collective-permute-start.2 = (bf16[16,6144]{1,0:T(8,128)(2,1)}, bf16[16,6144]{1,0:T(8,128)(2,1)}, u32[]{:S(2)}, u32[]{:S(2)}) collective-permute-start(bf16[16,6144]{1,0:T(8,128)(2,1)} %param.18), channel_id=1, source_target_pairs={{0,16},{1,17},{2,18},{3,19},{4,20},{5,21},{6,22},{7,23},{8,24},{9,... | collective-permute-start | bytes 589832 | tf_op jit(solution)/shard_map/ppermute | solution.py:347
  16.6 44.9 %copy-start.35 = (bf16[16,6144]{1,0:T(8,128)(2,1)S(1)}, bf16[16,6144]{1,0:T(8,128)(2,1)}, u32[]{:S(2)}) copy-start(bf16[16,6144]{1,0:T(8,128)(2,1)} %param.18) | copy-start | bytes 589828
  16.8 21.3 %copy-start.9 = (f32[4,96,384]{2,1,0:T(8,128)S(1)}, f32[4,96,384]{2,1,0:T(8,128)}, u32[]{:S(2)}) copy-start(f32[4,96,384]{2,1,0:T(8,128)} %get-tuple-element.82) | copy-start | bytes 1769476 | tf_op jit(solution)/shard_map/cond
  21.0 23.7 %copy-start.41 = (f32[32,8]{0,1:T(8,128)}, f32[32,8]{0,1:T(8,128)S(1)}, u32[]{:S(2)}) copy-start(f32[32,8]{0,1:T(8,128)S(1)} %convolution_multiply_fusion.1) | copy-start | bytes 3076 | tf_op jit(solution)/shard_map/cond
  27.7 17.0 %copy-start.13 = (f32[8,24576]{1,0:T(8,128)S(1)}, f32[8,24576]{1,0:T(8,128)}, u32[]{:S(2)}) copy-start(f32[8,24576]{1,0:T(8,128)} %get-tuple-element.83) | copy-start | bytes 2359300 | tf_op jit(solution)/shard_map/cond
  44.7 4.7 %copy-start.23 = (f32[8,6144]{1,0:T(8,128)S(1)}, f32[8,6144]{1,0:T(8,128)}, u32[]{:S(2)}) copy-start(f32[8,6144]{1,0:T(8,128)} %get-tuple-element.84) | copy-start | bytes 589828 | tf_op jit(solution)/shard_map/cond
  50.6 4.5 %copy-start.6 = (f32[4,96,384]{2,1,0:T(8,128)S(1)}, f32[4,96,384]{2,1,0:T(8,128)}, u32[]{:S(2)}) copy-start(f32[4,96,384]{2,1,0:T(8,128)} %get-tuple-element.85) | copy-start | bytes 1769476 | tf_op jit(solution)/shard_map/cond
  53.4 1.6 copy-start.19
  60.1 9.4 %copy-start.45 = (f32[32,1]{0,1:T(1,128)}, f32[32,1]{0,1:T(1,128)S(1)}, u32[]{:S(2)}) copy-start(f32[32,1]{0,1:T(1,128)S(1)} %get-tuple-element.135) | copy-start | bytes 388
  60.1 9.4 %collective-permute-start.1 = (bf16[32,6144]{1,0:T(8,128)(2,1)S(1)}, bf16[32,6144]{1,0:T(8,128)(2,1)S(1)}, u32[]{:S(2)}, u32[]{:S(2)}) collective-permute-start(bf16[32,6144]{1,0:T(8,128)(2,1)S(1)} %get-tuple-element.131), channel_id=1, source_target_pairs={{0,16},{1,17},{2,18},{3,19},{4,20},{5,21},{6,22},{7,23},{8,24},{9,... | collective-permute-start | bytes 1179656 | tf_op jit(solution)/shard_map/ppermute | solution.py:356
  71.5 97.5 %copy-start.28 = (bf16[32,6144]{1,0:T(8,128)(2,1)}, bf16[32,6144]{1,0:T(8,128)(2,1)S(1)}, u32[]{:S(2)}) copy-start(bf16[32,6144]{1,0:T(8,128)(2,1)S(1)} %get-tuple-element.132) | copy-start | bytes 1179652
  71.5 97.5 %collective-permute-start.4 = (bf16[32,6144]{1,0:T(8,128)(2,1)S(1)}, bf16[32,6144]{1,0:T(8,128)(2,1)S(1)}, u32[]{:S(2)}, u32[]{:S(2)}) collective-permute-start(bf16[32,6144]{1,0:T(8,128)(2,1)S(1)} %get-tuple-element.133), channel_id=1, source_target_pairs={{16,0},{17,1},{18,2},{19,3},{20,4},{21,5},{22,6},{23,7},{24,8},{25... | collective-permute-start | bytes 1179656 | tf_op jit(solution)/shard_map/ppermute | solution.py:368
  169.0 20.6 %copy-start.17 = (bf16[32,6144]{1,0:T(8,128)(2,1)}, bf16[32,6144]{1,0:T(8,128)(2,1)S(1)}, u32[]{:S(2)}) copy-start(bf16[32,6144]{1,0:T(8,128)(2,1)S(1)} %get-tuple-element.97) | copy-start | bytes 1179652 | tf_op jit(solution)/shard_map/cond
  169.0 20.0 %copy-start.8 = (f32[4,96,384]{2,1,0:T(8,128)S(1)}, f32[4,96,384]{2,1,0:T(8,128)}, u32[]{:S(2)}) copy-start(f32[4,96,384]{2,1,0:T(8,128)} %get-tuple-element.103) | copy-start | bytes 1769476 | tf_op jit(solution)/shard_map/cond
  189.9 3.6 %copy-start.3 = (f32[8,24576]{1,0:T(8,128)S(1)}, f32[8,24576]{1,0:T(8,128)}, u32[]{:S(2)}) copy-start(f32[8,24576]{1,0:T(8,128)} %get-tuple-element.105) | copy-start | bytes 2359300 | tf_op jit(solution)/shard_map/cond
  199.0 5.0 %copy-start.46 = (f32[32,1]{0,1:T(1,128)S(1)}, f32[32,1]{0,1:T(1,128)}, u32[]{:S(2)}) copy-start(f32[32,1]{0,1:T(1,128)} %get-tuple-element.98) | copy-start | bytes 388 | tf_op jit(solution)/shard_map/cond
  207.3 1.0 copy-start.12
  218.5 5.7 %copy-start.42 = (f32[32,8]{0,1:T(8,128)S(1)}, f32[32,8]{0,1:T(8,128)}, u32[]{:S(2)}) copy-start(f32[32,8]{0,1:T(8,128)} %get-tuple-element.110) | copy-start | bytes 3076 | tf_op jit(solution)/shard_map/cond
  226.1 2.6 copy-start.21
  226.1 3.5 %copy-start.34 = (f32[8,6144]{1,0:T(8,128)S(1)}, f32[8,6144]{1,0:T(8,128)}, u32[]{:S(2)}) copy-start(f32[8,6144]{1,0:T(8,128)} %fusion.222) | copy-start | bytes 589828 | tf_op jit(solution)/shard_map/cond
  226.1 4.2 %copy-start.30 = (f32[8,6144]{1,0:T(8,128)S(1)}, f32[8,6144]{1,0:T(8,128)}, u32[]{:S(2)}) copy-start(f32[8,6144]{1,0:T(8,128)} %fusion.242) | copy-start | bytes 589828 | tf_op jit(solution)/shard_map/cond
  226.1 5.8 %copy-start.27 = (f32[384,384]{1,0:T(8,128)S(1)}, f32[384,384]{1,0:T(8,128)}, u32[]{:S(2)}) copy-start(f32[384,384]{1,0:T(8,128)} %copy.33) | copy-start | bytes 1769476 | tf_op jit(solution)/shard_map/cond
  226.4 6.4 %copy-start.37 = (f32[6144]{0:T(1024)S(1)}, f32[6144]{0:T(1024)}, u32[]{:S(2)}) copy-start(f32[6144]{0:T(1024)} %get-tuple-element.161) | copy-start | bytes 73732 | tf_op jit(solution)/shard_map/cond
  226.4 7.1 %copy-start.18 = (bf16[32,6144]{1,0:T(8,128)(2,1)S(1)}, bf16[32,6144]{1,0:T(8,128)(2,1)}, u32[]{:S(2)}) copy-start(bf16[32,6144]{1,0:T(8,128)(2,1)} %get-tuple-element.249) | copy-start | bytes 1179652 | tf_op jit(solution)/shard_map/cond
  233.5 1.0 copy-start.29
  234.5 7.6 %collective-permute-start.3 = (bf16[16,6144]{1,0:T(8,128)(2,1)S(1)}, bf16[16,6144]{1,0:T(8,128)(2,1)S(1)}, u32[]{:S(2)}, u32[]{:S(2)}) collective-permute-start(bf16[16,6144]{1,0:T(8,128)(2,1)S(1)} %slice.311), channel_id=1, source_target_pairs={{16,0},{17,1},{18,2},{19,3},{20,4},{21,5},{22,6},{23,7},{24,8},{25... | collective-permute-start | bytes 589832 | tf_op jit(solution)/shard_map/ppermute | solution.py:369
  235.8 7.7 %collective-permute-start.5 = (bf16[16,6144]{1,0:T(8,128)(2,1)S(1)}, bf16[16,6144]{1,0:T(8,128)(2,1)S(1)}, u32[]{:S(2)}, u32[]{:S(2)}) collective-permute-start(bf16[16,6144]{1,0:T(8,128)(2,1)S(1)} %slice.314), channel_id=1, source_target_pairs={{0,16},{1,17},{2,18},{3,19},{4,20},{5,21},{6,22},{7,23},{8,24},{9,... | collective-permute-start | bytes 589832 | tf_op jit(solution)/shard_map/ppermute | solution.py:379
Sparse Core Ops, SparseCore 0:
  233.6 68.3 reduce-scatter.3

commit v2 on v1

--- a/solution.py
+++ b/solution.py
@@ -1,8 +1,11 @@
+import functools
 import math
 
 import jax
 import jax.numpy as jnp
 from jax import lax
+from jax.experimental import pallas as pl
+from jax.experimental.pallas import tpu as pltpu
 from jax.sharding import PartitionSpec as P
 
 precise = lax.Precision.HIGHEST
@@ -208,23 +211,6 @@
     )
 
 
-def matmul(a, b, ca, cb):
-    return lax.dot_general(
-        a, b, (((ca,), (cb,)), ((), ())),
-        precision=lax.Precision.HIGH, preferred_element_type=jnp.float32,
-    )
-
-
-def take_block(rows, index, width):
-    return lax.dynamic_slice_in_dim(rows, index * width, width, 1)
-
-
-def add_block(rows, part, index):
-    width = part.shape[1]
-    old = lax.dynamic_slice_in_dim(rows, index * width, width, 1)
-    return lax.dynamic_update_slice_in_dim(rows, old + part, index * width, 1)
-
-
 def masks(ranks, count):
     rank_index = jnp.arange(count, dtype=jnp.int32)
     return (
@@ -233,82 +219,238 @@
     )
 
 
-def forward_pass(rows, params, pattern, ranks):
+def parts(x):
+    high = x.astype(jnp.bfloat16).astype(jnp.float32)
+    return high, x - high
+
+
+def dot16(a, b, ca, cb):
+    return lax.dot_general(
+        a.astype(jnp.bfloat16), b.astype(jnp.bfloat16), (((ca,), (cb,)), ((), ())),
+        preferred_element_type=jnp.float32,
+    )
+
+
+def expand(a, b):
+    ah, al = parts(a)
+    bh, bl = parts(b)
+    return dot16(jnp.concatenate([ah, al, ah], 1), jnp.concatenate([bh, bh, bl], 0), 1, 0)
+
+
+def contract(a, b):
+    rows, count = a.shape[0], b.shape[0]
+    both = dot16(jnp.concatenate(parts(a), 0), jnp.concatenate(parts(b), 0), 1, 1)
+    return both[:rows, :count] + both[:rows, count:] + both[rows:, :count]
+
+
+def outer(a, b):
+    ah, al = parts(a)
+    bh, bl = parts(b)
+    return dot16(jnp.concatenate([ah, al, ah], 0), jnp.concatenate([bh, bh, bl], 0), 0, 0)
+
+
+def three(a, b, ca, cb):
+    ah, al = parts(a)
+    bh, bl = parts(b)
+    return dot16(ah, bh, ca, cb) + dot16(ah, bl, ca, cb) + dot16(al, bh, ca, cb)
+
+
+def span(index, width):
+    return pl.ds(pl.multiple_of(index * width, 128), width)
+
+
+def forward_kernel(
+    group, pattern, rows, up_wide, down_wide, up_left, up_right, down_left, down_right, gain, masks_ref,
+    out, scale_ref, low_ref, pre, low_down_ref, normed_ref, total,
+):
+    blocks, wide, hid = up_wide.shape
+    chunk = pre.shape[1] // 16
+    act = rows[...].astype(jnp.float32)
+    scale = lax.rsqrt(jnp.mean(act * act, axis=1, keepdims=True) + 1e-05)
+    scale_ref[...] = scale
+    normed = act * scale * gain[...]
+    normed_ref[...] = normed
+    low = contract(normed, up_left[...]) * masks_ref[0:1, :]
+    low_ref[...] = low
+
+    def fill(i, carry):
+        pre[:, span(i, chunk)] = expand(low, up_right[:, span(i, chunk)])
+        return carry
+
+    lax.fori_loop(0, 16, fill, 0)
+    for k in range(blocks):
+        source, target = pattern[k], pattern[blocks + k]
+        pre[:, span(target, hid)] += three(normed_ref[:, span(source // group, wide)], up_wide[k], 1, 0)
+
+    def sums(i, carry):
+        return carry + contract(gelu_tanh(pre[:, span(i, chunk)]), down_left[:, span(i, chunk)])
+
+    low_down = lax.fori_loop(0, 16, sums, jnp.zeros(low.shape, jnp.float32)) * masks_ref[1:2, :]
+    low_down_ref[...] = low_down
+    total[...] = act + expand(low_down, down_right[...])
+    for k in range(blocks):
+        source, target = pattern[2 * blocks + k], pattern[3 * blocks + k]
+        part = three(gelu_tanh(pre[:, span(source, hid)]), down_wide[k], 1, 1)
+        total[:, span(target // group, wide)] += part
+    out[...] = total[...].astype(jnp.bfloat16)
+
+
+def backward_kernel(
+    group, pattern, rows, upstream, scale_ref, low_ref, pre, low_down_ref,
+    up_wide, down_wide, up_left, up_right, down_left, down_right, gain, masks_ref,
+    act_grad, packed, g_up, g_down, normed_ref, grad_ref, d_pre, d_normed_ref,
+):
+    blocks, wide, hid = up_wide.shape
+    chunk = pre.shape[1] // 16
+    narrow = rows.shape[1] // 16
+    act = rows[...].astype(jnp.float32)
+    scale = scale_ref[...]
+    low = low_ref[...]
+    low_down = low_down_ref[...]
+    normed_ref[...] = act * scale * gain[...]
+    grad_ref[...] = upstream[...].astype(jnp.float32)
+    d_low_down = contract(grad_ref[...], down_right[...]) * masks_ref[1:2, :]
+
+    def fill(i, carry):
+        d_pre[:, span(i, chunk)] = expand(d_low_down, down_left[:, span(i, chunk)])
+        return carry
+
+    lax.fori_loop(0, 16, fill, 0)
+    for k in range(blocks):
+        source, target = pattern[2 * blocks + k], pattern[3 * blocks + k]
+        piece = grad_ref[:, span(target // group, wide)]
+        d_pre[:, span(source, hid)] += three(piece, down_wide[k], 1, 0)
+        g_down[k] = outer(gelu_tanh(pre[:, span(source, hid)]), piece)
+
+    def sums(i, carry):
+        here = span(i, chunk)
+        value = pre[:, here]
+        square = value * value
+        tanh = jnp.tanh(0.7978845608028654 * (value + 0.044715 * square * value))
+        half = 0.5 * (1.0 + tanh)
+        slope = half + 0.5 * value * (1.0 - tanh * tanh) * (
+            0.7978845608028654 * (1.0 + 3.0 * 0.044715 * square)
+        )
+        d_here = d_pre[:, here] * slope
+        d_pre[:, here] = d_here
+        packed[i, :, 0:chunk] = outer(low, d_here)
+        packed[i, :, chunk : 2 * chunk] = outer(d_low_down, value * half)
+        return carry + contract(d_here, up_right[:, here])
+
+    d_low = lax.fori_loop(0, 16, sums, jnp.zeros(low.shape, jnp.float32)) * masks_ref[0:1, :]
+    d_normed_ref[...] = expand(d_low, up_left[...])
+    for k in range(blocks):
+        source, target = pattern[k], pattern[blocks + k]
+        piece = d_pre[:, span(target, hid)]
+        here = span(source // group, wide)
+        d_normed_ref[:, here] += three(piece, up_wide[k], 1, 1)
+        g_up[k] = outer(piece, normed_ref[:, here])
+    d_normed = d_normed_ref[...]
+    unit = act * scale
+    scaled = d_normed * gain[...]
+    grad = grad_ref[...]
+    result = grad + scale * (scaled - unit * jnp.mean(scaled * unit, axis=1, keepdims=True))
+    act_grad[...] = result.astype(jnp.bfloat16)
+    g_gain = jnp.sum(d_normed * unit, axis=0, keepdims=True)
+    g_up_left = outer(d_low, normed_ref[...])
+    g_down_right = outer(low_down, grad)
+    base = 2 * chunk
+    for i in range(16):
+        cut = slice(i * narrow, (i + 1) * narrow)
+        packed[i, :, base : base + narrow] = g_up_left[:, cut]
+        packed[i, :, base + narrow : base + 2 * narrow] = g_down_right[:, cut]
+        packed[i, :, base + 2 * narrow :] = jnp.broadcast_to(g_gain[:, cut], (8, narrow))
+
+
+def local_call(body, count, shapes, scratch, cost):
+    vmem = pl.BlockSpec(memory_space=pltpu.VMEM)
+    return pl.pallas_call(
+        body,
+        in_specs=[pl.BlockSpec(memory_space=pltpu.SMEM)] + [vmem] * count,
+        out_specs=[vmem] * len(shapes),
+        out_shape=shapes,
+        scratch_shapes=scratch,
+        cost_estimate=pl.CostEstimate(flops=cost, bytes_accessed=8000000, transcendentals=800000),
+        compiler_params=pltpu.CompilerParams(vmem_limit_bytes=48 * 1024 * 1024),
+    )
+
+
+def widen(blocks, offsets, group):
+    chosen = offsets[:, None] % group == jnp.arange(group)[None, :]
+    wide = jnp.where(chosen[:, :, None, None], blocks[:, None], 0.0)
+    return wide.reshape(blocks.shape[0], group * blocks.shape[1], blocks.shape[2])
+
+
+def prepare(params, pattern, ranks):
     up_blocks, down_blocks, up_left, up_right, down_left, down_right, gain = params
-    act = rows.astype(jnp.float32)
-    blocks, feat, hid = up_blocks.shape
-    up_mask, down_mask = masks(ranks, up_left.shape[0])
-    scale = lax.rsqrt(jnp.mean(act * act, axis=1, keepdims=True) + 1e-05)
-    normed = act * scale * gain
-    low = matmul(normed, up_left, 1, 1) * up_mask
-    pre = matmul(low, up_right, 1, 0)
-    for k in range(blocks):
-        part = matmul(take_block(normed, pattern[0, 0, k], feat), up_blocks[k], 1, 0)
-        pre = add_block(pre, part, pattern[0, 1, k])
-    hidden = gelu_tanh(pre)
-    low_down = matmul(hidden, down_left, 1, 1) * down_mask
-    out = act + matmul(low_down, down_right, 1, 0)
-    for k in range(blocks):
-        part = matmul(take_block(hidden, pattern[1, 0, k], hid), down_blocks[k], 1, 1)
-        out = add_block(out, part, pattern[1, 1, k])
-    return out.astype(jnp.bfloat16), (scale, low, pre, low_down)
-
-
-def backward_pass(rows, upstream, saved, params, pattern, ranks, replicas):
-    up_blocks, down_blocks, up_left, up_right, down_left, down_right, gain = params
-    scale, low, pre, low_down = saved
-    act = rows.astype(jnp.float32)
-    grad = upstream.astype(jnp.float32)
-    blocks, feat, hid = up_blocks.shape
-    up_mask, down_mask = masks(ranks, up_left.shape[0])
-    unit = act * scale
-    normed = unit * gain
-    tanh = jnp.tanh(0.7978845608028654 * (pre + 0.044715 * pre * pre * pre))
-    hidden = 0.5 * pre * (1.0 + tanh)
-    slope = 0.5 * (1.0 + tanh) + 0.5 * pre * (1.0 - tanh * tanh) * (
-        0.7978845608028654 * (1.0 + 3.0 * 0.044715 * pre * pre)
-    )
-    d_low_down = matmul(grad, down_right, 1, 1) * down_mask
-    d_hidden = matmul(d_low_down, down_left, 1, 0)
-    g_down = []
-    for k in range(blocks):
-        piece = take_block(grad, pattern[1, 1, k], feat)
-        d_hidden = add_block(d_hidden, matmul(piece, down_blocks[k], 1, 0), pattern[1, 0, k])
-        g_down.append(matmul(take_block(hidden, pattern[1, 0, k], hid), piece, 0, 0))
-    d_pre = d_hidden * slope
-    d_low = matmul(d_pre, up_right, 1, 1) * up_mask
-    d_normed = matmul(d_low, up_left, 1, 0)
-    g_up = []
-    for k in range(blocks):
-        piece = take_block(d_pre, pattern[0, 1, k], hid)
-        d_normed = add_block(d_normed, matmul(piece, up_blocks[k], 1, 1), pattern[0, 0, k])
-        g_up.append(matmul(piece, take_block(normed, pattern[0, 0, k], feat), 0, 0))
-    scaled = d_normed * gain
-    act_grad = grad + scale * (scaled - unit * jnp.mean(scaled * unit, axis=1, keepdims=True))
-    g_gain = jnp.sum(d_normed * unit, axis=0)
-
-    def by_share(g):
-        return g.reshape(g.shape[0], replicas, -1).transpose(1, 0, 2)
-
-    def block_share(g):
-        whole = jnp.concatenate(g, axis=1)
+    group = 4
+    return (
+        widen(up_blocks, pattern[0, 0], group),
+        widen(down_blocks, pattern[1, 1], group),
+        up_left,
+        up_right,
+        down_left,
+        down_right,
+        gain[None],
+        jnp.stack(masks(ranks, up_left.shape[0])),
+    )
+
+
+def forward_pass(rows, ready, pattern):
+    count, width = rows.shape
+    rank, hidden = ready[3].shape
+    f32 = jnp.float32
+    shape = jax.ShapeDtypeStruct
+    out, scale, low, pre, low_down = local_call(
+        functools.partial(forward_kernel, 4),
+        9,
+        [
+            shape((count, width), jnp.bfloat16),
+            shape((count, 1), f32),
+            shape((count, rank), f32),
+            shape((count, hidden), f32),
+            shape((count, rank), f32),
+        ],
+        [pltpu.VMEM((count, width), f32), pltpu.VMEM((count, width), f32)],
+        100000000,
+    )(pattern.reshape(-1), rows, *ready)
+    return out, (scale, low, pre, low_down)
+
+
+def backward_pass(rows, upstream, saved, ready, pattern, replicas):
+    count, width = rows.shape
+    rank, hidden = ready[3].shape
+    blocks, wide, hid = ready[0].shape
+    f32 = jnp.float32
+    shape = jax.ShapeDtypeStruct
+    act_grad, packed, g_up, g_down = local_call(
+        functools.partial(backward_kernel, 4),
+        14,
+        [
+            shape((count, width), jnp.bfloat16),
+            shape((16, rank, (2 * hidden + 3 * width) // 16), f32),
+            shape((blocks, hid, wide), f32),
+            shape((blocks, hid, wide), f32),
+        ],
+        [
+            pltpu.VMEM((count, width), f32),
+            pltpu.VMEM((count, width), f32),
+            pltpu.VMEM((count, hidden), f32),
+            pltpu.VMEM((count, width), f32),
+        ],
+        200000000,
+    )(pattern.reshape(-1), rows, upstream, *saved, *ready)
+
+    def block_share(g, offsets):
+        chosen = offsets[:, None] % 4 == jnp.arange(4)[None, :]
+        cut = jnp.sum(jnp.where(chosen[:, None, :, None], g.reshape(blocks, hid, 4, -1), 0.0), axis=2)
+        whole = cut.transpose(1, 0, 2).reshape(hid, -1)
         eighths = whole.reshape(replicas, -1, 8, whole.shape[1]).transpose(0, 2, 1, 3)
         return eighths.reshape(replicas, 8, -1)
 
-    gain_rows = jnp.pad(g_gain.reshape(replicas, 1, -1), ((0, 0), (0, 7), (0, 0)))
-    packed = jnp.concatenate(
-        [
-            by_share(matmul(low, d_pre, 0, 0)),
-            by_share(matmul(d_low_down, hidden, 0, 0)),
-            by_share(matmul(d_low, normed, 0, 0)),
-            by_share(matmul(low_down, grad, 0, 0)),
-            block_share(g_up),
-            block_share(g_down),
-            gain_rows,
-        ],
-        axis=2,
-    )
-    return act_grad.astype(jnp.bfloat16), packed
+    return act_grad, jnp.concatenate(
+        [packed, block_share(g_up, pattern[0, 0]), block_share(g_down, pattern[1, 1])], axis=2
+    )
 
 
 def reduce_shares(packed):
@@ -342,12 +484,13 @@
     )
     pattern = block_pattern[0]
     ranks = rank_used[0]
+    ready = prepare(params, pattern, ranks)
     forth, back = [(0, 1)], [(1, 0)]
     first = jnp.concatenate([tokens, lax.ppermute(tokens, "pipe", back)], axis=0)
     top = jnp.concatenate([lax.ppermute(cotangent, "pipe", forth), cotangent], axis=0)
 
     def run(rows):
-        return forward_pass(rows, params, pattern, ranks)
+        return forward_pass(rows, ready, pattern)
 
     def skip_forward(rows):
         return jax.tree.map(lambda t: jnp.zeros(t.shape, t.dtype), jax.eval_shape(run, rows))
@@ -358,7 +501,7 @@
     def last(operands):
         rows, upstream = operands
         out, kept = run(rows)
-        below, packed = backward_pass(rows, upstream, kept, params, pattern, ranks, replicas)
+        below, packed = backward_pass(rows, upstream, kept, ready, pattern, replicas)
         return out, below, packed
 
     def skip_last(operands):
@@ -370,7 +513,7 @@
 
     def first_back(operands):
         upstream, kept, unused = operands
-        return backward_pass(first, upstream, kept, params, pattern, ranks, replicas)
+        return backward_pass(first, upstream, kept, ready, pattern, replicas)
 
     def skip_back(operands):
         return operands[0], operands[2]
@@ -387,7 +530,7 @@
     block_columns = hid // replicas // 8 * blocks * feat
     pieces = []
     start = 0
-    for extent in (hidden_share, hidden_share, width_share, width_share, block_columns, block_columns, width_share):
+    for extent in (hidden_share, hidden_share, width_share, width_share, width_share, block_columns, block_columns):
         pieces.append(share[:, start : start + extent])
         start += extent
 
@@ -398,13 +541,13 @@
     return (
         final_tokens,
         input_gradient,
-        unpack(pieces[4]),
         unpack(pieces[5]),
+        unpack(pieces[6]),
         pieces[2][None],
         pieces[0][None],
         pieces[1][None],
         pieces[3][None],
-        pieces[6][:1],
+        pieces[4][:1],
     )
 
 

time: 315 us -> 241 us (0.77)
  matrix products: 45.7 us -> 0 us
  waiting for transfers between devices: 165 us -> 132 us
  Pallas kernels: 0 us -> 32 us
  loops' own time: 20.8 us -> 0.05 us
  local copies, waits for them, and re-layouts: 33.1 us -> 26.4 us
    dot_general x36 -> x0, matrix products: 45.7 us -> none  [matmul(): lax.dot_general(a, b, (((ca,), (cb,)), ((), ())), precision=lax.Precision...]
    pallas_call x0 -> x2, Pallas kernels: none -> 32 us  [the longest x1 18.4 us: backward_pass(): local_call(functools.partial(backward_kernel, 4), 14, [shape((count, widt...]
    ppermute x1, waiting for transfers between devices: 96.2 us -> 67.5 us  [two_sections(): from_above = lax.ppermute(below, 'pipe', back)]
    another operation x1, loops' own time: 10.4 us -> 0.02 us  [two_sections(): result, saved = lax.cond(section == 0, run, skip_forward, first)]
    another operation x1, loops' own time: 10.4 us -> 0.03 us  [two_sections(): lax.cond(section == 0, first_back, skip_back, (from_above, saved, packed))]
    mul x4 -> x0, other arithmetic: 9.64 us -> none  [the longest x1 3.55 us: backward_pass(): hidden = 0.5 * pre * (1.0 + tanh)]
    dynamic_update_slice x8 -> x0, local copies, waits for them, and re-layouts: 7.67 us -> none  [add_block(): return lax.dynamic_update_slice_in_dim(rows, old + part, index * width, 1)]
    cond x42 -> x7, local copies, waits for them, and re-layouts: 9 us -> 2.37 us
  transfers between devices with their start and end apart: 7 -> 7, of which waited for: 6 -> 5; matrix products, arithmetic and copies ran while one was open for 11% -> 7% of each run, Pallas kernels for 0% -> 6%
where the time goes in v2:
time: 241 us
  waiting for transfers between devices  132 us (55%)
  Pallas kernels  32 us (13%)
  local copies, waits for them, and re-layouts  26.4 us (11%)
  other arithmetic  20.1 us (8%)
  starting transfers between devices  16 us (7%)
  between operations  14.2 us (6%)
    ppermute x1, waiting for transfers between devices, two_sections(): from_above = lax.ppermute(below, 'pipe', back)  67.5 us
    unnamed x2, waiting for transfers between devices  56.2 us
    pallas_call x1, Pallas kernels, backward_pass(): local_call(functools.partial(backward_kernel, 4), 14, [shape((count, widt...  18.4 us
    pallas_call x1, Pallas kernels, forward_pass(): local_call(functools.partial(forward_kernel, 4), 9, [shape((count, width)...  13.5 us
    ppermute x1, waiting for transfers between devices, two_sections(): second = lax.ppermute(result, 'pipe', forth)  6.86 us
    ppermute x1, starting transfers between devices, two_sections(): lax.ppermute(cotangent, 'pipe', forth)  6.19 us
    reduce_sum x2, other arithmetic, block_share(): jnp.sum(jnp.where(chosen[:, None, :, None], g.reshape(blocks, hid, 4, -1)...  5.76 us
    pallas_call x2, local copies, waits for them, and re-layouts, backward_pass(): local_call(functools.partial(backward_kernel, 4), 14, [shape((count, widt...  5.12 us
  transfers between devices with their start and end apart: 7, of which 5 were waited for; matrix products, arithmetic and copies ran while one was open for 7% of the time, Pallas kernels for 6%

profile of v2, /device:TPU:0, one launch (start us, length us, event | category | flops | bytes accessed | tf_op | source)
XLA Modules:
  0.0 240.7 jit_solution(10457208726419152102)
XLA Ops:
  7.2 1.3 collective-permute-start
  8.5 6.2 %collective-permute-start.2 = (bf16[16,6144]{1,0:T(8,128)(2,1)}, bf16[16,6144]{1,0:T(8,128)(2,1)}, u32[]{:S(2)}, u32[]{:S(2)}) collective-permute-start(bf16[16,6144]{1,0:T(8,128)(2,1)} %param.18), channel_id=1, source_target_pairs={{0,16},{1,17},{2,18},{3,19},{4,20},{5,21},{6,22},{7,23},{8,24},{9,... | collective-permute-start | bytes 589832 | tf_op jit(solution)/shard_map/ppermute | solution.py:490
  14.7 1.6 constant_dynamic-update-slice_fusion.1
  16.3 0.7 and_select_fusion.4
  17.4 1.3 fusion.7
  18.8 1.3 bitcast_select_fusion.1
  20.2 1.7 bitcast_select_fusion
  21.9 1.3 compare_select_fusion.12
  23.3 1.6 constant_dynamic-update-slice_fusion
  25.0 13.7 %conditional.3 = ((bf16[32,6144]{1,0:T(8,128)(2,1)}, f32[32,1]{1,0:T(8,128)}, f32[32,8]{1,0:T(8,128)}, f32[32,24576]{1,0:T(8,128)}, f32[32,8]{1,0:T(8,128)})) conditional(s32[]{:T(128)} %convert_element_type.8, () %tuple.31, (s32[1,2,2,4]{3,2,1,0:T(2,128)S(1)}, bf16[32,6144]{1,0:T(8,128)(2,1)}, f32[4,384,384]{2,1,0:T(8,128)S(1)}, ...), branch_computations={%region_0.1_spmd, %region_1.2_spmd} | conditional | flops 100000000 | bytes 8000136 | solution.py:498
  25.1 13.5 %branch_1_fun.4 = (bf16[32,6144]{1,0:T(8,128)(2,1)}, f32[32,1]{1,0:T(8,128)}, f32[32,8]{1,0:T(8,128)}, f32[32,24576]{1,0:T(8,128)}, f32[32,8]{1,0:T(8,128)}) custom-call(s32[16]{0:T(128)S(1)} %reshape_squeeze.6.pattern, bf16[32,6144]{1,0:T(8,128)(2,1)} %get-tuple-element.81.rows, f32[4,384,384]{2,1,0:T(8,128)S(1)} %get-tuple-element.82.up_wide, ...), custom_call_target="tpu_custom_call" | custom-call | flops 100000000 | bytes 8000000 | tf_op jit(solution)/shard_map/cond/branch_1_fun/pallas_call | solution.py:404
  38.6 1.3 collective-permute-start.1
  39.9 1.8 pad_maximum_fusion.2
  41.7 6.9 %collective-permute-done.1 = bf16[32,6144]{1,0:T(8,128)(2,1)S(1)} collective-permute-done((bf16[32,6144]{1,0:T(8,128)(2,1)}, bf16[32,6144]{1,0:T(8,128)(2,1)S(1)}, u32[]{:S(2)}, u32[]{:S(2)}) %collective-permute-start.1) | collective-permute-done | bytes 393248 | tf_op jit(solution)/shard_map/ppermute | solution.py:499
  48.6 3.5 %conditional.4 = (bf16[32,6144]{1,0:T(8,128)(2,1)}, bf16[32,6144]{1,0:T(8,128)(2,1)}, f32[16,8,6528]{2,1,0:T(8,128)}) conditional(s32[]{:T(128)} %convert_element_type.7, () %tuple.30, (s32[1,2,2,4]{3,2,1,0:T(2,128)S(1)}, bf16[32,6144]{1,0:T(8,128)(2,1)S(1)}, f32[4,384,384]{2,1,0:T(8,128)S(1)}, f32[4,384,384]{2,1,0:T(8,128)}, ...), branch_computations={%region_2.3_spmd, %region_3.6_spmd} | conditional | flops 303735680 | bytes 108897904 | solution.py:510
  48.6 0.8 broadcast.310
  49.4 0.8 broadcast.310.clone
  50.2 1.9 broadcast.311
  52.1 1.3 collective-permute-start.4
  53.4 67.5 %collective-permute-done.4 = bf16[32,6144]{1,0:T(8,128)(2,1)} collective-permute-done((bf16[32,6144]{1,0:T(8,128)(2,1)}, bf16[32,6144]{1,0:T(8,128)(2,1)}, u32[]{:S(2)}, u32[]{:S(2)}) %collective-permute-start.4) | collective-permute-done | bytes 393248 | tf_op jit(solution)/shard_map/ppermute | solution.py:511
  120.9 40.0 %conditional.5 = ((bf16[32,6144]{1,0:T(8,128)(2,1)}, f32[16,8,6528]{2,1,0:T(8,128)})) conditional(s32[]{:T(128)} %convert_element_type.8, (bf16[32,6144]{1,0:T(8,128)(2,1)}, f32[16,8,6528]{2,1,0:T(8,128)}) %tuple.34, (s32[1,2,2,4]{3,2,1,0:T(2,128)S(1)}, bf16[32,6144]{1,0:T(8,128)(2,1)}, bf16[32,6144]{1,0:T(8,128)(2,1)}, f32[32,1]{1,0:T(8,128)}, ...), branch_computations={%region_6.7_spmd, %region_7.10_spmd} | conditional | flops 203735680 | bytes 55186316 | solution.py:521
  120.9 1.0 copy.58.upstream
  121.9 18.4 %branch_1_fun.7 = (bf16[32,6144]{1,0:T(8,128)(2,1)}, f32[16,8,4224]{2,1,0:T(8,128)S(1)}, f32[4,384,384]{2,1,0:T(8,128)S(1)}, f32[4,384,384]{2,1,0:T(8,128)}) custom-call(s32[16]{0:T(128)S(1)} %reshape_squeeze.9.pattern, bf16[32,6144]{1,0:T(8,128)(2,1)} %get-tuple-element.112.rows, bf16[32,6144]{1,0:T(8,128)(2,1)S(1)} %copy.58.upstream, ...), custom_call_target="tpu_custom_call" | custom-call | flops 200000000 | bytes 8000000 | tf_op jit(solution)/shard_map/cond/branch_1_fun/pallas_call | solution.py:426
  140.4 1.4 copy-done.3
  141.7 3.1 %copy.32 = f32[4,384,384]{1,2,0:T(8,128)} copy(f32[4,384,384]{2,1,0:T(8,128)} %get-tuple-element.130) | data formatting | bytes 4718592 | tf_op jit(solution)/shard_map/cond/branch_1_fun/pallas_call | solution.py:426
  144.9 2.8 %select_reduce_fusion.2 = f32[4,384,96]{1,2,0:T(8,128)} fusion(f32[4,384,4,96]{1,3,2,0:T(8,128)} %bitcast.79, pred[4,4]{1,0:T(4,128)(4,1)S(1)} %get-tuple-element.184), kind=kLoop, calls=%fused_computation.14 | loop fusion | flops 1032192 | bytes 2949136 | tf_op jit(solution)/shard_map/cond/branch_1_fun/reduce_sum | solution.py:446
  147.7 1.4 copy.33
  149.0 1.2 reshape.382
  150.2 2.1 copy.30
  152.3 3.0 %select_reduce_fusion.3 = f32[4,384,96]{1,2,0:T(8,128)} fusion(f32[4,384,4,96]{1,3,2,0:T(8,128)} %bitcast.81, pred[4,4]{1,0:T(4,128)(4,1)S(1)} %get-tuple-element.185), kind=kLoop, calls=%fused_computation.15 | loop fusion | flops 1032192 | bytes 2949136 | tf_op jit(solution)/shard_map/cond/branch_1_fun/reduce_sum | solution.py:446
  155.3 1.4 copy.31
  156.6 1.2 reshape.379
  157.9 3.0 %pad_maximum_fusion.1 = f32[16,8,6528]{2,1,0:T(8,128)} fusion(f32[16,8,1152]{2,1,0:T(8,128)S(1)} %bitcast.88, f32[16,8,1152]{2,1,0:T(8,128)} %bitcast.90, f32[16,8,4224]{2,1,0:T(8,128)S(1)} %copy-done.4), kind=kLoop, calls=%fused_computation.13 | loop fusion | flops 1671168 | bytes 6684672 | tf_op jit(solution)/shard_map/cond/branch_1_fun/concatenate | solution.py:451
  160.9 0.9 slice.65
  161.8 1.3 collective-permute-start.3
  163.1 0.9 slice.68
  164.1 4.6 %collective-permute-start.5 = (bf16[16,6144]{1,0:T(8,128)(2,1)S(1)}, bf16[16,6144]{1,0:T(8,128)(2,1)S(1)}, u32[]{:S(2)}, u32[]{:S(2)}) collective-permute-start(bf16[16,6144]{1,0:T(8,128)(2,1)S(1)} %slice.68), channel_id=1, source_target_pairs={{0,16},{1,17},{2,18},{3,19},{4,20},{5,21},{6,22},{7,23},{8,24},{9,... | collective-permute-start | bytes 589832 | tf_op jit(solution)/shard_map/ppermute | solution.py:522
  168.6 0.7 collective-permute-done.3
  169.4 1.6 slice_select_fusion.1
  171.0 0.8 collective-permute-done.5
  171.8 1.6 slice_select_fusion
  173.4 56.2 %reduce-scatter.4.cloned.1.call-done = f32[1,8,6528]{2,1,0:T(8,128)} async-done(((f32[16,8,6528]{2,1,0:T(8,128)}), f32[1,8,6528]{2,1,0:T(8,128)}) %reduce-scatter.4.cloned.1.call-update) | async-done | bytes 208912
  229.6 1.0 multiply_bitcast_fusion
  230.6 0.6 slice_bitcast_fusion.2
  231.2 0.6 slice_bitcast_fusion
  231.8 0.6 slice.84
  232.5 0.6 copy.34
  233.2 0.6 copy.35
  (34 shorter events, 0.9 us)
Async XLA Ops:
  7.2 222.5 %reduce-scatter.4.cloned.1.call-start = ((), (), s32[]{:S(2)}) async-start(), calls=%async_computation.1 | async-start | bytes 3551232
  7.2 16.1 %collective-permute-start = (bf16[16,6144]{1,0:T(8,128)(2,1)}, bf16[16,6144]{1,0:T(8,128)(2,1)}, u32[]{:S(2)}, u32[]{:S(2)}) collective-permute-start(bf16[16,6144]{1,0:T(8,128)(2,1)} %param.17), channel_id=1, source_target_pairs={{16,0},{17,1},{18,2},{19,3},{20,4},{21,5},{22,6},{23,7},{24,8},{25... | collective-permute-start | bytes 589832 | tf_op jit(solution)/shard_map/ppermute | solution.py:489
  8.5 31.4 %collective-permute-start.2 = (bf16[16,6144]{1,0:T(8,128)(2,1)}, bf16[16,6144]{1,0:T(8,128)(2,1)}, u32[]{:S(2)}, u32[]{:S(2)}) collective-permute-start(bf16[16,6144]{1,0:T(8,128)(2,1)} %param.18), channel_id=1, source_target_pairs={{0,16},{1,17},{2,18},{3,19},{4,20},{5,21},{6,22},{7,23},{8,24},{9,... | collective-permute-start | bytes 589832 | tf_op jit(solution)/shard_map/ppermute | solution.py:490
  17.4 2.7 %copy-start.17 = (f32[1,4,96,384]{3,2,1,0:T(8,128)S(1)}, f32[1,4,96,384]{3,2,1,0:T(8,128)}, u32[]{:S(2)}) copy-start(f32[1,4,96,384]{3,2,1,0:T(8,128)} %param.21) | copy-start | bytes 1769476
  20.1 28.5 %copy-start.5 = (f32[4,384,384]{2,1,0:T(8,128)}, f32[4,384,384]{2,1,0:T(8,128)S(1)}, u32[]{:S(2)}) copy-start(f32[4,384,384]{2,1,0:T(8,128)S(1)} %bitcast_select_fusion.1) | copy-start | bytes 7077892
  20.1 4.8 %copy-start.9 = (f32[1,8,24576]{2,1,0:T(8,128)S(1)}, f32[1,8,24576]{2,1,0:T(8,128)}, u32[]{:S(2)}) copy-start(f32[1,8,24576]{2,1,0:T(8,128)} %param.23) | copy-start | bytes 2359300
  20.1 4.8 %copy-start.11 = (f32[1,8,6144]{2,1,0:T(8,128)S(1)}, f32[1,8,6144]{2,1,0:T(8,128)}, u32[]{:S(2)}) copy-start(f32[1,8,6144]{2,1,0:T(8,128)} %param.22) | copy-start | bytes 589828
  20.2 4.8 %copy-start.12 = (f32[1,8,6144]{2,1,0:T(8,128)S(1)}, f32[1,8,6144]{2,1,0:T(8,128)}, u32[]{:S(2)}) copy-start(f32[1,8,6144]{2,1,0:T(8,128)} %param.25) | copy-start | bytes 589828
  20.2 4.8 %copy-start.19 = (s32[1,2,2,4]{3,2,1,0:T(2,128)S(1)}, s32[1,2,2,4]{3,2,1,0:T(2,128)}, u32[]{:S(2)}) copy-start(s32[1,2,2,4]{3,2,1,0:T(2,128)} %param.26) | copy-start | bytes 196
  38.6 10.0 %collective-permute-start.1 = (bf16[32,6144]{1,0:T(8,128)(2,1)}, bf16[32,6144]{1,0:T(8,128)(2,1)S(1)}, u32[]{:S(2)}, u32[]{:S(2)}) collective-permute-start(bf16[32,6144]{1,0:T(8,128)(2,1)} %get-tuple-element.150), channel_id=1, source_target_pairs={{0,16},{1,17},{2,18},{3,19},{4,20},{5,21},{6,22},{7,23},{8,24},{9,... | collective-permute-start | bytes 1179656 | tf_op jit(solution)/shard_map/ppermute | solution.py:499
  52.1 68.8 %collective-permute-start.4 = (bf16[32,6144]{1,0:T(8,128)(2,1)}, bf16[32,6144]{1,0:T(8,128)(2,1)}, u32[]{:S(2)}, u32[]{:S(2)}) collective-permute-start(bf16[32,6144]{1,0:T(8,128)(2,1)} %get-tuple-element.152), channel_id=1, source_target_pairs={{16,0},{17,1},{18,2},{19,3},{20,4},{21,5},{22,6},{23,7},{24,8},{25... | collective-permute-start | bytes 1179656 | tf_op jit(solution)/shard_map/ppermute | solution.py:511
  140.3 1.4 copy-start.3
  152.3 5.6 %copy-start.4 = (f32[16,8,4224]{2,1,0:T(8,128)S(1)}, f32[16,8,4224]{2,1,0:T(8,128)}, u32[]{:S(2)}) copy-start(f32[16,8,4224]{2,1,0:T(8,128)} %copy-done.3) | copy-start | bytes 6488068 | tf_op jit(solution)/shard_map/cond
  152.3 5.6 %copy-start.13 = (f32[16,3,8,384]{3,2,1,0:T(8,128)S(1)}, f32[16,3,8,384]{3,2,1,0:T(8,128)}, u32[]{:S(2)}) copy-start(f32[16,3,8,384]{3,2,1,0:T(8,128)} %reshape.382) | copy-start | bytes 1769476 | tf_op jit(solution)/shard_map/cond
  161.8 7.6 %collective-permute-start.3 = (bf16[16,6144]{1,0:T(8,128)(2,1)S(1)}, bf16[16,6144]{1,0:T(8,128)(2,1)S(1)}, u32[]{:S(2)}, u32[]{:S(2)}) collective-permute-start(bf16[16,6144]{1,0:T(8,128)(2,1)S(1)} %slice.65), channel_id=1, source_target_pairs={{16,0},{17,1},{18,2},{19,3},{20,4},{21,5},{22,6},{23,7},{24,8},{25... | collective-permute-start | bytes 589832 | tf_op jit(solution)/shard_map/ppermute | solution.py:512
  164.1 7.7 %collective-permute-start.5 = (bf16[16,6144]{1,0:T(8,128)(2,1)S(1)}, bf16[16,6144]{1,0:T(8,128)(2,1)S(1)}, u32[]{:S(2)}, u32[]{:S(2)}) collective-permute-start(bf16[16,6144]{1,0:T(8,128)(2,1)S(1)} %slice.68), channel_id=1, source_target_pairs={{0,16},{1,17},{2,18},{3,19},{4,20},{5,21},{6,22},{7,23},{8,24},{9,... | collective-permute-start | bytes 589832 | tf_op jit(solution)/shard_map/ppermute | solution.py:522
Sparse Core Ops, SparseCore 0:
  161.0 68.5 reduce-scatter.3

commit v3 on v2

--- a/solution.py
+++ b/solution.py
@@ -417,7 +417,7 @@
     return out, (scale, low, pre, low_down)
 
 
-def backward_pass(rows, upstream, saved, ready, pattern, replicas):
+def backward_pass(rows, upstream, saved, ready, pattern):
     count, width = rows.shape
     rank, hidden = ready[3].shape
     blocks, wide, hid = ready[0].shape
@@ -441,6 +441,13 @@
         200000000,
     )(pattern.reshape(-1), rows, upstream, *saved, *ready)
 
+    return act_grad, (packed, g_up, g_down)
+
+
+def pack(grads, pattern, replicas):
+    packed, g_up, g_down = grads
+    blocks, hid = g_up.shape[:2]
+
     def block_share(g, offsets):
         chosen = offsets[:, None] % 4 == jnp.arange(4)[None, :]
         cut = jnp.sum(jnp.where(chosen[:, None, :, None], g.reshape(blocks, hid, 4, -1), 0.0), axis=2)
@@ -448,7 +455,7 @@
         eighths = whole.reshape(replicas, -1, 8, whole.shape[1]).transpose(0, 2, 1, 3)
         return eighths.reshape(replicas, 8, -1)
 
-    return act_grad, jnp.concatenate(
+    return jnp.concatenate(
         [packed, block_share(g_up, pattern[0, 0]), block_share(g_down, pattern[1, 1])], axis=2
     )
 
@@ -501,7 +508,7 @@
     def last(operands):
         rows, upstream = operands
         out, kept = run(rows)
-        below, packed = backward_pass(rows, upstream, kept, ready, pattern, replicas)
+        below, packed = backward_pass(rows, upstream, kept, ready, pattern)
         return out, below, packed
 
     def skip_last(operands):
@@ -513,7 +520,7 @@
 
     def first_back(operands):
         upstream, kept, unused = operands
-        return backward_pass(first, upstream, kept, ready, pattern, replicas)
+        return backward_pass(first, upstream, kept, ready, pattern)
 
     def skip_back(operands):
         return operands[0], operands[2]
@@ -523,7 +530,7 @@
     final_tokens = jnp.where(section == 0, final_early, final[count:])
     input_gradient = jnp.where(section == 0, bottom[:count], bottom_late)
     factor = 1.0 / math.sqrt(count * 2 * replicas)
-    share = reduce_shares(packed) * factor
+    share = reduce_shares(pack(packed, pattern, replicas)) * factor
     blocks, feat, hid = params[0].shape
     hidden_share = params[3].shape[1] // replicas
     width_share = width // replicas

time: 241 us -> 205 us (0.85)
  waiting for transfers between devices: 132 us -> 101 us
  other arithmetic: 20.1 us -> 16.1 us
    ppermute x1, waiting for transfers between devices: 67.5 us -> 35.9 us  [two_sections(): from_above = lax.ppermute(below, 'pipe', back)]
    another operation x3 -> x9, local copies, waits for them, and re-layouts: 3.49 us -> 11.1 us
    pallas_call x2 -> x0, local copies, waits for them, and re-layouts: 5.12 us -> none  [backward_pass(): local_call(functools.partial(backward_kernel, 4), 14, [shape((count, widt...]
    reduce_sum x2, other arithmetic: 5.76 us -> 1.32 us  [block_share(): jnp.sum(jnp.where(chosen[:, None, :, None], g.reshape(blocks, hid, 4, -1)...]
    reshape x2 -> x0, local copies, waits for them, and re-layouts: 2.43 us -> none  [block_share(): whole.reshape(replicas, -1, 8, whole.shape[1]).transpose(0, 2, 1, 3)]
  transfers between devices with their start and end apart: 7 -> 7, of which waited for: 5 -> 5; matrix products, arithmetic and copies ran while one was open for 7% -> 8% of each run, Pallas kernels for 6% -> 7%
where the time goes in v3:
time: 205 us; the launch traced here: 204 us
  waiting for transfers between devices  101 us (49%)
  Pallas kernels  32.7 us (16%)
  local copies, waits for them, and re-layouts  24.9 us (12%)
  other arithmetic  16.1 us (8%)
  starting transfers between devices  16 us (8%)
  between operations  14.3 us (7%)
    unnamed x2, waiting for transfers between devices  56.2 us
    ppermute x1, waiting for transfers between devices, two_sections(): from_above = lax.ppermute(below, 'pipe', back)  35.9 us
    pallas_call x1, Pallas kernels, backward_pass(): local_call(functools.partial(backward_kernel, 4), 14, [shape((count, widt...  19.2 us
    pallas_call x1, Pallas kernels, forward_pass(): local_call(functools.partial(forward_kernel, 4), 9, [shape((count, width)...  13.6 us
    another operation x7, local copies, waits for them, and re-layouts  10.3 us
    ppermute x1, waiting for transfers between devices, two_sections(): second = lax.ppermute(result, 'pipe', forth)  6.85 us
    ppermute x1, starting transfers between devices, two_sections(): lax.ppermute(cotangent, 'pipe', forth)  6.19 us
    ppermute x1, starting transfers between devices, two_sections(): bottom_late = lax.ppermute(bottom[count:], 'pipe', forth)  4.57 us
  transfers between devices with their start and end apart: 7, of which 5 were waited for; matrix products, arithmetic and copies ran while one was open for 8% of the time, Pallas kernels for 7%

profile of v3, /device:TPU:0, one launch (start us, length us, event | category | flops | bytes accessed | tf_op | source)
XLA Modules:
  0.0 204.5 jit_solution(17621900603935234674)
XLA Ops:
  7.2 1.3 collective-permute-start
  8.5 6.2 %collective-permute-start.2 = (bf16[16,6144]{1,0:T(8,128)(2,1)}, bf16[16,6144]{1,0:T(8,128)(2,1)}, u32[]{:S(2)}, u32[]{:S(2)}) collective-permute-start(bf16[16,6144]{1,0:T(8,128)(2,1)} %param.18), channel_id=1, source_target_pairs={{0,16},{1,17},{2,18},{3,19},{4,20},{5,21},{6,22},{7,23},{8,24},{9,... | collective-permute-start | bytes 589832 | tf_op jit(solution)/shard_map/ppermute | solution.py:497
  14.7 1.6 constant_dynamic-update-slice_fusion.1
  16.3 1.3 fusion.3
  17.6 0.7 and_select_fusion
  18.9 1.4 bitcast_select_fusion.1
  20.4 1.7 bitcast_select_fusion
  22.1 1.3 compare_select_fusion.4
  23.5 1.6 constant_dynamic-update-slice_fusion
  25.1 13.7 %conditional.3 = ((bf16[32,6144]{1,0:T(8,128)(2,1)}, f32[32,1]{1,0:T(8,128)}, f32[32,8]{1,0:T(8,128)}, f32[32,24576]{1,0:T(8,128)}, f32[32,8]{1,0:T(8,128)})) conditional(s32[]{:T(128)} %convert_element_type.8, () %tuple.44, (s32[1,2,2,4]{3,2,1,0:T(2,128)S(1)}, bf16[32,6144]{1,0:T(8,128)(2,1)}, f32[4,384,384]{2,1,0:T(8,128)S(1)}, ...), branch_computations={%region_0.1_spmd, %region_1.2_spmd} | conditional | flops 100000000 | bytes 8000136 | solution.py:505
  25.2 13.6 %branch_1_fun.4 = (bf16[32,6144]{1,0:T(8,128)(2,1)}, f32[32,1]{1,0:T(8,128)}, f32[32,8]{1,0:T(8,128)}, f32[32,24576]{1,0:T(8,128)}, f32[32,8]{1,0:T(8,128)}) custom-call(s32[16]{0:T(128)S(1)} %reshape_squeeze.6.pattern, bf16[32,6144]{1,0:T(8,128)(2,1)} %get-tuple-element.109.rows, f32[4,384,384]{2,1,0:T(8,128)S(1)} %get-tuple-element.110.up_wide, ...), custom_call_target="tpu_custom_call" | custom-call | flops 100000000 | bytes 8000000 | tf_op jit(solution)/shard_map/cond/branch_1_fun/pallas_call | solution.py:404
  38.8 1.3 collective-permute-start.1
  40.1 1.8 pad_maximum_fusion.1
  41.9 6.8 %collective-permute-done.1 = bf16[32,6144]{1,0:T(8,128)(2,1)S(1)} collective-permute-done((bf16[32,6144]{1,0:T(8,128)(2,1)}, bf16[32,6144]{1,0:T(8,128)(2,1)S(1)}, u32[]{:S(2)}, u32[]{:S(2)}) %collective-permute-start.1) | collective-permute-done | bytes 393248 | tf_op jit(solution)/shard_map/ppermute | solution.py:506
  48.8 6.3 %conditional.4 = (bf16[32,6144]{1,0:T(8,128)(2,1)}, bf16[32,6144]{1,0:T(8,128)(2,1)}, f32[16,8,4224]{2,1,0:T(8,128)}, f32[4,384,384]{2,1,0:T(8,128)}, f32[4,384,384]{2,1,0:T(8,128)}) conditional(s32[]{:T(128)} %convert_element_type.7, () %tuple.43, (s32[1,2,2,4]{3,2,1,0:T(2,128)S(1)}, bf16[32,6144]{1,0:T(8,128)(2,1)S(1)}, ...), branch_computations={%region_2.3_spmd, %region_3.4_spmd} | conditional | flops 300000000 | bytes 33400144 | solution.py:517
  48.8 0.8 broadcast.180.clone
  49.5 0.8 broadcast.180
  50.3 1.5 broadcast.181
  51.8 1.6 broadcast.182.clone
  53.5 1.6 broadcast.182
  55.0 1.3 collective-permute-start.4
  56.3 35.9 %collective-permute-done.4 = bf16[32,6144]{1,0:T(8,128)(2,1)} collective-permute-done((bf16[32,6144]{1,0:T(8,128)(2,1)}, bf16[32,6144]{1,0:T(8,128)(2,1)}, u32[]{:S(2)}, u32[]{:S(2)}) %collective-permute-start.4) | collective-permute-done | bytes 393248 | tf_op jit(solution)/shard_map/ppermute | solution.py:518
  92.2 21.0 %conditional.5 = ((bf16[32,6144]{1,0:T(8,128)(2,1)}, f32[16,8,4224]{2,1,0:T(8,128)}, f32[4,384,384]{2,1,0:T(8,128)}, f32[4,384,384]{2,1,0:T(8,128)})) conditional(s32[]{:T(128)} %convert_element_type.8, (bf16[32,6144]{1,0:T(8,128)(2,1)}, f32[16,8,4224]{2,1,0:T(8,128)}, f32[4,384,384]{2,1,0:T(8,128)}, f32[4,384,384]{2,1,0:T(8,128)}) %tuple.47, ...), branch_computations={%region_4.5_spmd, %region_5.6_spmd} | conditional | flops 200000000 | bytes 10359488 | solution.py:528
  92.2 0.7 copy-done.4
  93.0 1.0 copy.66.upstream
  94.1 19.2 %branch_1_fun.7 = (bf16[32,6144]{1,0:T(8,128)(2,1)}, f32[16,8,4224]{2,1,0:T(8,128)}, f32[4,384,384]{2,1,0:T(8,128)}, f32[4,384,384]{2,1,0:T(8,128)}) custom-call(s32[16]{0:T(128)S(1)} %reshape_squeeze.9.pattern, bf16[32,6144]{1,0:T(8,128)(2,1)} %get-tuple-element.139.rows, bf16[32,6144]{1,0:T(8,128)(2,1)S(1)} %copy.66.upstream, ...), custom_call_target="tpu_custom_call" | custom-call | flops 200000000 | bytes 8000000 | tf_op jit(solution)/shard_map/cond/branch_1_fun/pallas_call | solution.py:426
  113.2 2.0 copy.34
  115.9 0.4 reshape_reshape.7
  116.2 2.0 copy.35
  118.3 1.1 select_reduce_fusion.1
  119.4 1.4 copy.30
  120.7 0.4 reshape_reshape.6
  121.1 3.5 %pad_maximum_fusion = f32[16,8,6528]{2,1,0:T(8,128)} fusion(f32[16,8,1152]{2,1,0:T(8,128)S(1)} %bitcast.68, f32[16,8,1152]{2,1,0:T(8,128)S(1)} %bitcast.69, f32[16,8,4224]{2,1,0:T(8,128)} %get-tuple-element.227), kind=kLoop, calls=%fused_computation | loop fusion | flops 1671168 | bytes 6684672 | tf_op jit(solution)/shard_map/concatenate | solution.py:458
  124.7 0.9 slice.55
  125.6 1.3 collective-permute-start.3
  126.9 0.9 slice.58
  127.9 4.6 %collective-permute-start.5 = (bf16[16,6144]{1,0:T(8,128)(2,1)S(1)}, bf16[16,6144]{1,0:T(8,128)(2,1)S(1)}, u32[]{:S(2)}, u32[]{:S(2)}) collective-permute-start(bf16[16,6144]{1,0:T(8,128)(2,1)S(1)} %slice.58), channel_id=1, source_target_pairs={{0,16},{1,17},{2,18},{3,19},{4,20},{5,21},{6,22},{7,23},{8,24},{9,... | collective-permute-start | bytes 589832 | tf_op jit(solution)/shard_map/ppermute | solution.py:529
  132.4 0.7 collective-permute-done.3
  133.2 1.6 slice_select_fusion.1
  134.8 0.8 collective-permute-done.5
  135.6 1.6 slice_select_fusion
  137.2 56.2 %reduce-scatter.4.cloned.1.call-done = f32[1,8,6528]{2,1,0:T(8,128)} async-done(((f32[16,8,6528]{2,1,0:T(8,128)}), f32[1,8,6528]{2,1,0:T(8,128)}) %reduce-scatter.4.cloned.1.call-update) | async-done | bytes 208912
  193.4 1.0 multiply_bitcast_fusion
  194.4 0.6 slice.74
  195.0 0.6 slice_bitcast_fusion.2
  195.6 0.6 slice_bitcast_fusion
  196.3 0.6 copy.32
  197.0 0.6 copy.33
  (34 shorter events, 1.7 us)
Async XLA Ops:
  7.2 186.3 %reduce-scatter.4.cloned.1.call-start = ((), (), s32[]{:S(2)}) async-start(), calls=%async_computation.1 | async-start | bytes 3551232
  7.2 16.2 %collective-permute-start = (bf16[16,6144]{1,0:T(8,128)(2,1)}, bf16[16,6144]{1,0:T(8,128)(2,1)}, u32[]{:S(2)}, u32[]{:S(2)}) collective-permute-start(bf16[16,6144]{1,0:T(8,128)(2,1)} %param.17), channel_id=1, source_target_pairs={{16,0},{17,1},{18,2},{19,3},{20,4},{21,5},{22,6},{23,7},{24,8},{25... | collective-permute-start | bytes 589832 | tf_op jit(solution)/shard_map/ppermute | solution.py:496
  8.5 31.6 %collective-permute-start.2 = (bf16[16,6144]{1,0:T(8,128)(2,1)}, bf16[16,6144]{1,0:T(8,128)(2,1)}, u32[]{:S(2)}, u32[]{:S(2)}) collective-permute-start(bf16[16,6144]{1,0:T(8,128)(2,1)} %param.18), channel_id=1, source_target_pairs={{0,16},{1,17},{2,18},{3,19},{4,20},{5,21},{6,22},{7,23},{8,24},{9,... | collective-permute-start | bytes 589832 | tf_op jit(solution)/shard_map/ppermute | solution.py:497
  18.4 0.5 copy-start.13
  18.9 1.5 copy-start.10
  20.4 4.7 %copy-start.1 = (f32[1,8,24576]{2,1,0:T(8,128)S(1)}, f32[1,8,24576]{2,1,0:T(8,128)}, u32[]{:S(2)}) copy-start(f32[1,8,24576]{2,1,0:T(8,128)} %param.23) | copy-start | bytes 2359300
  20.4 4.7 %copy-start.3 = (f32[1,8,6144]{2,1,0:T(8,128)S(1)}, f32[1,8,6144]{2,1,0:T(8,128)}, u32[]{:S(2)}) copy-start(f32[1,8,6144]{2,1,0:T(8,128)} %param.22) | copy-start | bytes 589828
  20.4 4.7 %copy-start.5 = (f32[1,8,6144]{2,1,0:T(8,128)S(1)}, f32[1,8,6144]{2,1,0:T(8,128)}, u32[]{:S(2)}) copy-start(f32[1,8,6144]{2,1,0:T(8,128)} %param.25) | copy-start | bytes 589828
  20.4 4.7 %copy-start.12 = (s32[1,2,2,4]{3,2,1,0:T(2,128)S(1)}, s32[1,2,2,4]{3,2,1,0:T(2,128)}, u32[]{:S(2)}) copy-start(s32[1,2,2,4]{3,2,1,0:T(2,128)} %param.26) | copy-start | bytes 196
  38.8 10.0 %collective-permute-start.1 = (bf16[32,6144]{1,0:T(8,128)(2,1)}, bf16[32,6144]{1,0:T(8,128)(2,1)S(1)}, u32[]{:S(2)}, u32[]{:S(2)}) collective-permute-start(bf16[32,6144]{1,0:T(8,128)(2,1)} %get-tuple-element.176), channel_id=1, source_target_pairs={{0,16},{1,17},{2,18},{3,19},{4,20},{5,21},{6,22},{7,23},{8,24},{9,... | collective-permute-start | bytes 1179656 | tf_op jit(solution)/shard_map/ppermute | solution.py:506
  55.0 37.2 %collective-permute-start.4 = (bf16[32,6144]{1,0:T(8,128)(2,1)}, bf16[32,6144]{1,0:T(8,128)(2,1)}, u32[]{:S(2)}, u32[]{:S(2)}) collective-permute-start(bf16[32,6144]{1,0:T(8,128)(2,1)} %get-tuple-element.178), channel_id=1, source_target_pairs={{16,0},{17,1},{18,2},{19,3},{20,4},{21,5},{22,6},{23,7},{24,8},{25... | collective-permute-start | bytes 1179656 | tf_op jit(solution)/shard_map/ppermute | solution.py:518
  92.2 0.7 copy-start.4
  92.2 0.7 copy-start.6
  113.2 2.1 %copy-start.14 = (pred[4,4]{1,0:T(4,128)(4,1)S(1)}, pred[4,4]{1,0:T(4,128)(4,1)}, u32[]{:S(2)}) copy-start(pred[4,4]{1,0:T(4,128)(4,1)} %copy-done.13) | copy-start | bytes 52
  125.6 7.6 %collective-permute-start.3 = (bf16[16,6144]{1,0:T(8,128)(2,1)S(1)}, bf16[16,6144]{1,0:T(8,128)(2,1)S(1)}, u32[]{:S(2)}, u32[]{:S(2)}) collective-permute-start(bf16[16,6144]{1,0:T(8,128)(2,1)S(1)} %slice.55), channel_id=1, source_target_pairs={{16,0},{17,1},{18,2},{19,3},{20,4},{21,5},{22,6},{23,7},{24,8},{25... | collective-permute-start | bytes 589832 | tf_op jit(solution)/shard_map/ppermute | solution.py:519
  127.9 7.7 %collective-permute-start.5 = (bf16[16,6144]{1,0:T(8,128)(2,1)S(1)}, bf16[16,6144]{1,0:T(8,128)(2,1)S(1)}, u32[]{:S(2)}, u32[]{:S(2)}) collective-permute-start(bf16[16,6144]{1,0:T(8,128)(2,1)S(1)} %slice.58), channel_id=1, source_target_pairs={{0,16},{1,17},{2,18},{3,19},{4,20},{5,21},{6,22},{7,23},{8,24},{9,... | collective-permute-start | bytes 589832 | tf_op jit(solution)/shard_map/ppermute | solution.py:529
Sparse Core Ops, SparseCore 0:
  124.8 68.5 reduce-scatter.3

commit v4 on v3

--- a/solution.py
+++ b/solution.py
@@ -461,7 +461,8 @@
 
 
 def reduce_shares(packed):
-    return lax.psum_scatter(packed, "dp", scatter_dimension=0, tiled=False)
+    sent = lax.all_to_all(packed.astype(jnp.bfloat16), "dp", 0, 0, tiled=True)
+    return jnp.sum(sent.astype(jnp.float32), axis=0)
 
 
 def two_sections(

time: 205 us -> 167 us (0.81)
  the two profiles are of different devices: /device:TPU:0 before, /device:TPU:13 now
where the time goes in v4:
time: 167 us; the launch traced here: 166 us
  waiting for transfers between devices  68.6 us (41%)
  Pallas kernels  32.7 us (20%)
  local copies, waits for them, and re-layouts  25.2 us (15%)
  starting transfers between devices  22.9 us (14%)
  other arithmetic  15.8 us (9%)
    ppermute x1, waiting for transfers between devices, two_sections(): from_above = lax.ppermute(below, 'pipe', back)  34.9 us
    all_to_all x1, waiting for transfers between devices, reduce_shares(): sent = lax.all_to_all(packed.astype(jnp.bfloat16), 'dp', 0, 0, tiled=True)  25.9 us
    pallas_call x1, Pallas kernels, backward_pass(): local_call(functools.partial(backward_kernel, 4), 14, [shape((count, widt...  19.2 us
    pallas_call x1, Pallas kernels, forward_pass(): local_call(functools.partial(forward_kernel, 4), 9, [shape((count, width)...  13.6 us
    another operation x7, local copies, waits for them, and re-layouts  10.3 us
    all_to_all x1, starting transfers between devices, reduce_shares(): sent = lax.all_to_all(packed.astype(jnp.bfloat16), 'dp', 0, 0, tiled=True)  8.39 us
    ppermute x1, waiting for transfers between devices, two_sections(): second = lax.ppermute(result, 'pipe', forth)  5.91 us
    ppermute x1, starting transfers between devices, two_sections(): lax.ppermute(cotangent, 'pipe', forth)  5.32 us
  transfers between devices with their start and end apart: 7, of which 5 were waited for; matrix products, arithmetic and copies ran while one was open for 10% of the time, Pallas kernels for 8%

profile of v4, /device:TPU:13, one launch (start us, length us, event | category | flops | bytes accessed | tf_op | source)
XLA Modules:
  0.0 166.1 jit_solution(2278065798224082024)
XLA Ops:
  0.6 1.3 collective-permute-start
  1.9 5.3 %collective-permute-start.2 = (bf16[16,6144]{1,0:T(8,128)(2,1)}, bf16[16,6144]{1,0:T(8,128)(2,1)}, u32[]{:S(2)}, u32[]{:S(2)}) collective-permute-start(bf16[16,6144]{1,0:T(8,128)(2,1)} %param.18), channel_id=1, source_target_pairs={{0,16},{1,17},{2,18},{3,19},{4,20},{5,21},{6,22},{7,23},{8,24},{9,... | collective-permute-start | bytes 589832 | tf_op jit(solution)/shard_map/ppermute | solution.py:498
  7.3 1.6 constant_dynamic-update-slice_fusion.1
  8.9 1.3 fusion.3
  10.2 0.7 and_select_fusion
  11.5 1.4 bitcast_select_fusion.1
  13.0 1.7 %bitcast_select_fusion = f32[4,384,384]{2,1,0:T(8,128)} fusion(f32[4,96,384]{2,1,0:T(8,128)S(1)} %bitcast.74, pred[4,384]{1,0:T(4,128)(4,1)S(1)} %broadcast_in_dim.109), kind=kLoop, calls=%fused_computation.1 | loop fusion | flops 589824 | bytes 2950656 | tf_op jit(solution)/shard_map/jit(_where)/select_n | solution.py:380
  14.7 1.3 compare_select_fusion.4
  16.0 1.6 constant_dynamic-update-slice_fusion
  17.6 13.7 %conditional.3 = ((bf16[32,6144]{1,0:T(8,128)(2,1)}, f32[32,1]{1,0:T(8,128)}, f32[32,8]{1,0:T(8,128)}, f32[32,24576]{1,0:T(8,128)}, f32[32,8]{1,0:T(8,128)})) conditional(s32[]{:T(128)} %convert_element_type.12, () %tuple.44, (s32[1,2,2,4]{3,2,1,0:T(2,128)S(1)}, bf16[32,6144]{1,0:T(8,128)(2,1)}, f32[4,384,384]{2,1,0:T(8,128)S(1)}, ...), branch_computations={%region_0.1_spmd, %region_1.2_spmd} | conditional | flops 100000000 | bytes 8000136 | solution.py:506
  17.7 13.6 %branch_1_fun.4 = (bf16[32,6144]{1,0:T(8,128)(2,1)}, f32[32,1]{1,0:T(8,128)}, f32[32,8]{1,0:T(8,128)}, f32[32,24576]{1,0:T(8,128)}, f32[32,8]{1,0:T(8,128)}) custom-call(s32[16]{0:T(128)S(1)} %reshape_squeeze.6.pattern, bf16[32,6144]{1,0:T(8,128)(2,1)} %get-tuple-element.109.rows, f32[4,384,384]{2,1,0:T(8,128)S(1)} %get-tuple-element.110.up_wide, ...), custom_call_target="tpu_custom_call" | custom-call | flops 100000000 | bytes 8000000 | tf_op jit(solution)/shard_map/cond/branch_1_fun/pallas_call | solution.py:404
  31.3 1.3 collective-permute-start.1
  32.6 1.8 %pad_maximum_fusion.1 = bf16[32,6144]{1,0:T(8,128)(2,1)} fusion(bf16[16,6144]{1,0:T(8,128)(2,1)} %param.18, bf16[16,6144]{1,0:T(8,128)(2,1)} %collective-permute-done.2), kind=kLoop, calls=%fused_computation.6 | loop fusion | flops 786432 | bytes 786432 | tf_op jit(solution)/shard_map/concatenate | solution.py:498
  34.4 5.9 %collective-permute-done.1 = bf16[32,6144]{1,0:T(8,128)(2,1)S(1)} collective-permute-done((bf16[32,6144]{1,0:T(8,128)(2,1)}, bf16[32,6144]{1,0:T(8,128)(2,1)S(1)}, u32[]{:S(2)}, u32[]{:S(2)}) %collective-permute-start.1) | collective-permute-done | bytes 393248 | tf_op jit(solution)/shard_map/ppermute | solution.py:507
  40.3 6.3 %conditional.4 = (bf16[32,6144]{1,0:T(8,128)(2,1)}, bf16[32,6144]{1,0:T(8,128)(2,1)}, f32[16,8,4224]{2,1,0:T(8,128)}, f32[4,384,384]{2,1,0:T(8,128)}, f32[4,384,384]{2,1,0:T(8,128)}) conditional(s32[]{:T(128)} %convert_element_type.11, () %tuple.43, (s32[1,2,2,4]{3,2,1,0:T(2,128)S(1)}, bf16[32,6144]{1,0:T(8,128)(2,1)S(1)}, ...), branch_computations={%region_2.3_spmd, %region_3.4_spmd} | conditional | flops 300000000 | bytes 33400144 | solution.py:518
  40.3 0.8 broadcast.178.clone
  41.1 0.8 broadcast.178
  41.9 1.5 broadcast.179
  43.4 1.6 broadcast.180.clone
  45.0 1.6 broadcast.180
  46.6 1.3 collective-permute-start.4
  47.9 34.9 %collective-permute-done.4 = bf16[32,6144]{1,0:T(8,128)(2,1)} collective-permute-done((bf16[32,6144]{1,0:T(8,128)(2,1)}, bf16[32,6144]{1,0:T(8,128)(2,1)}, u32[]{:S(2)}, u32[]{:S(2)}) %collective-permute-start.4) | collective-permute-done | bytes 393248 | tf_op jit(solution)/shard_map/ppermute | solution.py:519
  82.8 21.0 %conditional.5 = ((bf16[32,6144]{1,0:T(8,128)(2,1)}, f32[16,8,4224]{2,1,0:T(8,128)}, f32[4,384,384]{2,1,0:T(8,128)}, f32[4,384,384]{2,1,0:T(8,128)})) conditional(s32[]{:T(128)} %convert_element_type.12, (bf16[32,6144]{1,0:T(8,128)(2,1)}, f32[16,8,4224]{2,1,0:T(8,128)}, f32[4,384,384]{2,1,0:T(8,128)}, f32[4,384,384]{2,1,0:T(8,128)}) %tuple.47, ...), branch_computations={%region_4.5_spmd, %region_5.6_spmd} | conditional | flops 200000000 | bytes 10359488 | solution.py:529
  82.8 0.7 copy-done.4
  83.5 1.0 copy.66.upstream
  84.6 19.2 %branch_1_fun.7 = (bf16[32,6144]{1,0:T(8,128)(2,1)}, f32[16,8,4224]{2,1,0:T(8,128)}, f32[4,384,384]{2,1,0:T(8,128)}, f32[4,384,384]{2,1,0:T(8,128)}) custom-call(s32[16]{0:T(128)S(1)} %reshape_squeeze.9.pattern, bf16[32,6144]{1,0:T(8,128)(2,1)} %get-tuple-element.139.rows, bf16[32,6144]{1,0:T(8,128)(2,1)S(1)} %copy.66.upstream, ...), custom_call_target="tpu_custom_call" | custom-call | flops 200000000 | bytes 8000000 | tf_op jit(solution)/shard_map/cond/branch_1_fun/pallas_call | solution.py:426
  103.8 2.0 %copy.34 = f32[4,384,384]{1,2,0:T(8,128)S(1)} copy(f32[4,384,384]{2,1,0:T(8,128)} %get-tuple-element.230) | data formatting | bytes 4718592 | tf_op jit(solution)/shard_map
  106.3 1.0 reshape_reshape.9
  107.4 1.7 %convert.22 = bf16[16,8,4224]{2,1,0:T(8,128)(2,1)S(1)} convert(f32[16,8,4224]{2,1,0:T(8,128)} %get-tuple-element.228) | non-fusion elementwise | flops 540672 | bytes 3244032 | tf_op jit(solution)/shard_map/convert
  109.1 2.0 %copy.35 = f32[4,384,384]{1,2,0:T(8,128)S(1)} copy(f32[4,384,384]{2,1,0:T(8,128)} %get-tuple-element.229) | data formatting | bytes 4718592 | tf_op jit(solution)/shard_map
  111.1 1.0 select_reduce_fusion.1
  112.1 1.2 copy.30
  113.3 0.3 reshape_reshape.8
  113.6 2.3 %pad_maximum_fusion = bf16[16,8,6528]{2,1,0:T(8,128)(2,1)} fusion(bf16[16,8,1152]{2,1,0:T(8,128)(2,1)} %bitcast.69, bf16[16,8,1152]{2,1,0:T(8,128)(2,1)S(1)} %bitcast.70, bf16[16,8,4224]{2,1,0:T(8,128)(2,1)S(1)} %convert.22), kind=kLoop, calls=%fused_computation.5 | loop fusion | flops 5013504 | bytes 3342336 | tf_op jit(solution)/shard_map/concatenate | solution.py:458
  115.9 8.4 %all-to-all-start = ((bf16[16,8,6528]{2,1,0:T(8,128)(2,1)}), bf16[16,8,6528]{2,1,0:T(8,128)(2,1)S(1)}, u32[]{:S(2)}, u32[]{:S(2)}) async-start(bf16[16,8,6528]{2,1,0:T(8,128)(2,1)} %pad_maximum_fusion), calls=%async_computation | async-start | bytes 3342336 | tf_op jit(solution)/shard_map/all_to_all | solution.py:464
  124.3 0.9 slice.55
  125.2 1.3 collective-permute-start.3
  126.5 0.9 slice.58
  127.5 4.0 %collective-permute-start.5 = (bf16[16,6144]{1,0:T(8,128)(2,1)S(1)}, bf16[16,6144]{1,0:T(8,128)(2,1)S(1)}, u32[]{:S(2)}, u32[]{:S(2)}) collective-permute-start(bf16[16,6144]{1,0:T(8,128)(2,1)S(1)} %slice.58), channel_id=1, source_target_pairs={{0,16},{1,17},{2,18},{3,19},{4,20},{5,21},{6,22},{7,23},{8,24},{9,... | collective-permute-start | bytes 589832 | tf_op jit(solution)/shard_map/ppermute | solution.py:530
  131.5 1.8 %collective-permute-done.3 = bf16[16,6144]{1,0:T(8,128)(2,1)S(1)} collective-permute-done((bf16[16,6144]{1,0:T(8,128)(2,1)S(1)}, bf16[16,6144]{1,0:T(8,128)(2,1)S(1)}, u32[]{:S(2)}, u32[]{:S(2)}) %collective-permute-start.3) | collective-permute-done | bytes 196640 | tf_op jit(solution)/shard_map/ppermute | solution.py:520
  133.2 1.6 slice_select_fusion.1
  135.1 1.6 slice_select_fusion
  136.7 25.9 %all-to-all-done = bf16[16,8,6528]{2,1,0:T(8,128)(2,1)S(1)} async-done(((bf16[16,8,6528]{2,1,0:T(8,128)(2,1)}), bf16[16,8,6528]{2,1,0:T(8,128)(2,1)S(1)}, u32[]{:S(2)}, u32[]{:S(2)}) %all-to-all-start) | async-done | bytes 1671200 | tf_op jit(solution)/shard_map/all_to_all | solution.py:464
  162.8 0.6 slice.74
  163.4 0.6 slice_bitcast_fusion.2
  164.0 0.6 slice_bitcast_fusion
  164.7 0.6 copy.32
  165.5 0.6 copy.33
  (35 shorter events, 2.0 us)
Async XLA Ops:
  0.6 15.3 %collective-permute-start = (bf16[16,6144]{1,0:T(8,128)(2,1)}, bf16[16,6144]{1,0:T(8,128)(2,1)}, u32[]{:S(2)}, u32[]{:S(2)}) collective-permute-start(bf16[16,6144]{1,0:T(8,128)(2,1)} %param.17), channel_id=1, source_target_pairs={{16,0},{17,1},{18,2},{19,3},{20,4},{21,5},{22,6},{23,7},{24,8},{25... | collective-permute-start | bytes 589832 | tf_op jit(solution)/shard_map/ppermute | solution.py:497
  1.9 30.7 %collective-permute-start.2 = (bf16[16,6144]{1,0:T(8,128)(2,1)}, bf16[16,6144]{1,0:T(8,128)(2,1)}, u32[]{:S(2)}, u32[]{:S(2)}) collective-permute-start(bf16[16,6144]{1,0:T(8,128)(2,1)} %param.18), channel_id=1, source_target_pairs={{0,16},{1,17},{2,18},{3,19},{4,20},{5,21},{6,22},{7,23},{8,24},{9,... | collective-permute-start | bytes 589832 | tf_op jit(solution)/shard_map/ppermute | solution.py:498
  11.0 0.5 copy-start.13
  11.5 1.5 copy-start.10
  12.9 4.7 %copy-start.1 = (f32[1,8,24576]{2,1,0:T(8,128)S(1)}, f32[1,8,24576]{2,1,0:T(8,128)}, u32[]{:S(2)}) copy-start(f32[1,8,24576]{2,1,0:T(8,128)} %param.23) | copy-start | bytes 2359300
  12.9 4.7 %copy-start.3 = (f32[1,8,6144]{2,1,0:T(8,128)S(1)}, f32[1,8,6144]{2,1,0:T(8,128)}, u32[]{:S(2)}) copy-start(f32[1,8,6144]{2,1,0:T(8,128)} %param.22) | copy-start | bytes 589828
  12.9 4.7 %copy-start.5 = (f32[1,8,6144]{2,1,0:T(8,128)S(1)}, f32[1,8,6144]{2,1,0:T(8,128)}, u32[]{:S(2)}) copy-start(f32[1,8,6144]{2,1,0:T(8,128)} %param.25) | copy-start | bytes 589828
  12.9 4.7 %copy-start.12 = (s32[1,2,2,4]{3,2,1,0:T(2,128)S(1)}, s32[1,2,2,4]{3,2,1,0:T(2,128)}, u32[]{:S(2)}) copy-start(s32[1,2,2,4]{3,2,1,0:T(2,128)} %param.26) | copy-start | bytes 196
  31.3 9.0 %collective-permute-start.1 = (bf16[32,6144]{1,0:T(8,128)(2,1)}, bf16[32,6144]{1,0:T(8,128)(2,1)S(1)}, u32[]{:S(2)}, u32[]{:S(2)}) collective-permute-start(bf16[32,6144]{1,0:T(8,128)(2,1)} %get-tuple-element.176), channel_id=1, source_target_pairs={{0,16},{1,17},{2,18},{3,19},{4,20},{5,21},{6,22},{7,23},{8,24},{9,... | collective-permute-start | bytes 1179656 | tf_op jit(solution)/shard_map/ppermute | solution.py:507
  46.6 36.2 %collective-permute-start.4 = (bf16[32,6144]{1,0:T(8,128)(2,1)}, bf16[32,6144]{1,0:T(8,128)(2,1)}, u32[]{:S(2)}, u32[]{:S(2)}) collective-permute-start(bf16[32,6144]{1,0:T(8,128)(2,1)} %get-tuple-element.178), channel_id=1, source_target_pairs={{16,0},{17,1},{18,2},{19,3},{20,4},{21,5},{22,6},{23,7},{24,8},{25... | collective-permute-start | bytes 1179656 | tf_op jit(solution)/shard_map/ppermute | solution.py:519
  82.8 0.7 copy-start.4
  82.8 0.7 copy-start.6
  103.8 2.1 %copy-start.14 = (pred[4,4]{1,0:T(4,128)(4,1)S(1)}, pred[4,4]{1,0:T(4,128)(4,1)}, u32[]{:S(2)}) copy-start(pred[4,4]{1,0:T(4,128)(4,1)} %copy-done.13) | copy-start | bytes 52
  115.9 46.7 %all-to-all-start = ((bf16[16,8,6528]{2,1,0:T(8,128)(2,1)}), bf16[16,8,6528]{2,1,0:T(8,128)(2,1)S(1)}, u32[]{:S(2)}, u32[]{:S(2)}) async-start(bf16[16,8,6528]{2,1,0:T(8,128)(2,1)} %pad_maximum_fusion), calls=%async_computation | async-start | bytes 3342336 | tf_op jit(solution)/shard_map/all_to_all | solution.py:464
  125.2 8.0 %collective-permute-start.3 = (bf16[16,6144]{1,0:T(8,128)(2,1)S(1)}, bf16[16,6144]{1,0:T(8,128)(2,1)S(1)}, u32[]{:S(2)}, u32[]{:S(2)}) collective-permute-start(bf16[16,6144]{1,0:T(8,128)(2,1)S(1)} %slice.55), channel_id=1, source_target_pairs={{16,0},{17,1},{18,2},{19,3},{20,4},{21,5},{22,6},{23,7},{24,8},{25... | collective-permute-start | bytes 589832 | tf_op jit(solution)/shard_map/ppermute | solution.py:520
  127.5 7.6 %collective-permute-start.5 = (bf16[16,6144]{1,0:T(8,128)(2,1)S(1)}, bf16[16,6144]{1,0:T(8,128)(2,1)S(1)}, u32[]{:S(2)}, u32[]{:S(2)}) collective-permute-start(bf16[16,6144]{1,0:T(8,128)(2,1)S(1)} %slice.58), channel_id=1, source_target_pairs={{0,16},{1,17},{2,18},{3,19},{4,20},{5,21},{6,22},{7,23},{8,24},{9,... | collective-permute-start | bytes 589832 | tf_op jit(solution)/shard_map/ppermute | solution.py:530
